TPU v7x, 256 devices: a whole 4x4x8 slice. The times are simulated.
256 devices in a mesh: freq: 16 (over y_hi, x, core), recv: 16 (over y_lo, z).
Axes of the slice: x: 4, y: 4 (y_hi: 2, y_lo: 2; y = y_hi * 2 + y_lo), z: 8, core: 2. Of those that a mesh axis runs over, the one named last changes fastest.
Arguments:
- response: bfloat16 [2, 256, 512, 4096], P(None, 'freq', 'recv'), may hold values from -0.0625 to 0.0625
- focusing: float32 [2, 256, 16, 4096], P(None, 'freq', None, 'recv'), may hold values from -6 to 6
- window_onset: int32 [16, 512], P(None, ('recv', 'freq')), may hold values from 0 to 511
- window_end: int32 [16, 512], P(None, ('recv', 'freq')), may hold values from 128 to 1023, as said below
Outputs:
- windowed: float32 [16, 512, 1024], P(None, ('recv', 'freq'))
Inputs may be any that keep to these rules, and one draw needn't show every extreme that they name: window_end - window_onset lies between 128 and 512 for every trace.
All inputs are finite; a program needn't handle non-finite values.
Results may differ from a plain program's by a relative error of at most 0.0029.
Values may be sent and summed in bfloat16 or wider, within the bound.
No kernel may reach another device: no remote copies, remote signals or barrier semaphores. Data moves between devices by JAX's collectives and lax.ppermute only.
A program may use at most 64 MiB of HBM per device.

v0:
```python
import math

import jax
import jax.numpy as jnp
from jax import lax
from jax.sharding import PartitionSpec as P

NF = 256
NT = 1024


def make_table(count):
    freqs = jnp.arange(count, dtype=jnp.int32)
    samples = jnp.arange(NT, dtype=jnp.int32)
    phase = (freqs[:, None] * samples[None, :] % NT).astype(jnp.float32) * (2.0 * math.pi / NT)
    scale = 1.0 / math.sqrt(NF)
    return jnp.concatenate([jnp.cos(phase) * scale, -jnp.sin(phase) * scale], 0)


def transform(stacked, table):
    return lax.dot_general(
        stacked,
        table,
        (((0,), (0,)), ((), ())),
        precision=lax.Precision.HIGHEST,
        preferred_element_type=jnp.float32,
    )


def per_device(response, focusing, window_onset, window_end):
    focal = focusing.shape[2]
    focus_half = focusing.astype(jnp.bfloat16)
    gathered = lax.all_gather(focus_half, "recv", axis=3, tiled=True)
    real_part = jnp.einsum(
        "krs,kqs->krq", response[0], gathered[0], preferred_element_type=jnp.float32
    )
    real_part = real_part - jnp.einsum(
        "krs,kqs->krq", response[1], gathered[1], preferred_element_type=jnp.float32
    )
    imag_part = jnp.einsum(
        "krs,kqs->krq", response[0], gathered[1], preferred_element_type=jnp.float32
    )
    imag_part = imag_part + jnp.einsum(
        "krs,kqs->krq", response[1], gathered[0], preferred_element_type=jnp.float32
    )
    spectra = jnp.stack([real_part, imag_part])
    owned = window_onset.shape[1]
    moved = lax.all_to_all(spectra, "freq", split_axis=2, concat_axis=1, tiled=True)
    flat = moved.reshape(2 * NF, owned * focal)
    traces = transform(flat, make_table(NF))
    traces = jnp.transpose(traces.reshape(owned, focal, NT), (1, 0, 2))
    samples = jnp.arange(NT, dtype=jnp.int32)
    keep = (samples[None, None, :] >= window_onset[:, :, None]) & (
        samples[None, None, :] < window_end[:, :, None]
    )
    return jnp.where(keep, traces, jnp.float32(0.0))


def solution(mesh):
    in_specs = (
        P(None, "freq", "recv", None),
        P(None, "freq", None, "recv"),
        P(None, ("recv", "freq")),
        P(None, ("recv", "freq")),
    )
    out_specs = P(None, ("recv", "freq"), None)
    return jax.shard_map(
        per_device, mesh=mesh, in_specs=in_specs, out_specs=out_specs, check_vma=False
    )
```

profile of v0, /device:TPU:1, one launch (start us, length us, event | category | flops | bytes accessed | tf_op | source)
XLA Modules:
  0.0 139.6 jit_solution(12699561626764175694)
XLA Ops:
  6.5 0.0 all-gather.2.cloned.1.call-start
  6.5 1.8 %convert_element_type.8 = bf16[2,16,16,256]{3,2,1,0:T(8,128)(2,1)} convert(f32[2,16,16,256]{3,2,1,0:T(8,128)} %param.5) | non-fusion elementwise | flops 131072 | bytes 786432 | tf_op jit(solution)/shard_map/convert_element_type | solution.py:32
  8.3 0.0 all-gather.2.cloned.1.call-update
  8.3 84.3 %all-gather.2.cloned.1.call-done = bf16[2,16,16,4096]{3,2,1,0:T(8,128)(2,1)} async-done(((bf16[2,16,16,256]{3,2,1,0:T(8,128)(2,1)}), bf16[2,16,16,4096]{3,2,1,0:T(8,128)(2,1)}) %all-gather.2.cloned.1.call-update) | async-done | bytes 4194320 | tf_op jit(solution)/shard_map/all_gather | solution.py:33
  92.7 0.0 copy-start.2
  92.7 4.2 %fusion.2 = f32[16,32,16]{1,2,0:T(8,128)S(1)} fusion(bf16[2,16,32,4096]{3,2,1,0:T(8,128)(2,1)} %param.4, bf16[2,16,16,4096]{3,2,1,0:T(8,128)(2,1)} %all-gather.2.cloned.1.call-done), kind=kOutput, calls=%fused_computation.2 | convolution fusion | flops 67108864 | bytes 6324224 | tf_op jit(solution)/shard_map/krs,kqs->krq/dot_general | solution.py:37
  96.9 1.0 copy-done.2
  97.9 0.0 copy-start.3
  97.9 2.9 %fusion = f32[16,32,16]{1,2,0:T(8,128)S(1)} fusion(bf16[2,16,32,4096]{3,2,1,0:T(8,128)(2,1)S(1)} %copy-done.2, bf16[2,16,16,4096]{3,2,1,0:T(8,128)(2,1)} %all-gather.2.cloned.1.call-done), kind=kOutput, calls=%fused_computation | convolution fusion | flops 67108864 | bytes 6324224 | tf_op jit(solution)/shard_map/krs,kqs->krq/dot_general | solution.py:43
  100.8 0.0 copy-done.3
  100.8 1.2 fusion.20
  102.1 1.2 fusion.26
  103.3 0.0 copy-start
  103.3 0.0 copy-start.1
  103.3 0.5 copy.9
  103.8 0.9 reshape.10
  104.7 16.5 %all-to-all-start = ((f32[16,1,1024]{2,1,0:T(1,128)}), f32[16,1,1024]{2,1,0:T(1,128)S(1)}, u32[]{:S(2)}, u32[]{:S(2)}) async-start(f32[16,1,1024]{2,1,0:T(1,128)} %reshape.10), calls=%async_computation | async-start | bytes 131072 | tf_op jit(solution)/shard_map/all_to_all | solution.py:48
  121.1 4.1 %negate_multiply_fusion = (f32[256,1024]{1,0:T(8,128)S(1)}, f32[256,1024]{1,0:T(8,128)S(1)}) fusion(), kind=kLoop, calls=%fused_computation.30 | loop fusion | flops 4456448 | bytes 2097152 | tf_op jit(solution)/shard_map/mul | solution.py:17
  125.3 3.2 %all-to-all-done = f32[16,1,1024]{2,1,0:T(1,128)S(1)} async-done(((f32[16,1,1024]{2,1,0:T(1,128)}), f32[16,1,1024]{2,1,0:T(1,128)S(1)}, u32[]{:S(2)}, u32[]{:S(2)}) %all-to-all-start) | async-done | bytes 65568 | tf_op jit(solution)/shard_map/all_to_all | solution.py:48
  128.5 0.5 broadcast.20
  129.0 0.8 reduce
  129.8 0.2 reshape.11
  130.0 0.4 copy.11
  130.4 0.3 reshape.8
  130.7 0.0 copy-done
  130.7 0.0 copy-done.1
  130.7 1.3 fusion.16
  132.0 0.8 copy.12
  (1 shorter events, 0.0 us)
Async XLA Ops:
  6.5 86.1 %all-gather.2.cloned.1.call-start = ((), (), s32[]{:S(2)}) async-start(), calls=%async_computation.1 | async-start | bytes 4456448 | tf_op jit(solution)/shard_map/all_gather | solution.py:33
  92.7 5.2 %copy-start.2 = (bf16[2,16,32,4096]{3,2,1,0:T(8,128)(2,1)S(1)}, bf16[2,16,32,4096]{3,2,1,0:T(8,128)(2,1)}, u32[]{:S(2)}) copy-start(bf16[2,16,32,4096]{3,2,1,0:T(8,128)(2,1)} %param.4) | copy-start | bytes 25165828
  97.9 2.9 %copy-start.3 = (bf16[2,16,16,4096]{3,2,1,0:T(8,128)(2,1)S(1)}, bf16[2,16,16,4096]{3,2,1,0:T(8,128)(2,1)}, u32[]{:S(2)}) copy-start(bf16[2,16,16,4096]{3,2,1,0:T(8,128)(2,1)} %all-gather.2.cloned.1.call-done) | copy-start | bytes 12582916
  103.3 27.4 %copy-start = (s32[16,2]{0,1:T(2,128)S(1)}, s32[16,2]{0,1:T(2,128)}, u32[]{:S(2)}) copy-start(s32[16,2]{0,1:T(2,128)} %param.7) | copy-start | bytes 388
  103.3 27.4 %copy-start.1 = (s32[16,2]{0,1:T(2,128)S(1)}, s32[16,2]{0,1:T(2,128)}, u32[]{:S(2)}) copy-start(s32[16,2]{0,1:T(2,128)} %param.6) | copy-start | bytes 388
  104.7 23.8 %all-to-all-start = ((f32[16,1,1024]{2,1,0:T(1,128)}), f32[16,1,1024]{2,1,0:T(1,128)S(1)}, u32[]{:S(2)}, u32[]{:S(2)}) async-start(f32[16,1,1024]{2,1,0:T(1,128)} %reshape.10), calls=%async_computation | async-start | bytes 131072 | tf_op jit(solution)/shard_map/all_to_all | solution.py:48
Sparse Core Ops, SparseCore 0:
  9.1 83.5 all-gather.1
where the time goes:
time: 140 us
  waiting for transfers between devices  87.5 us (62%)
  starting transfers between devices  16.5 us (12%)
  between operations  13.5 us (10%)
  matrix products  10.9 us (8%)
  other arithmetic  6.75 us (5%)
  local copies, waits for them, and re-layouts  4.55 us (3%)
    all_gather x1, waiting for transfers between devices, per_device(): gathered = lax.all_gather(focus_half, 'recv', axis=3, tiled=True)  84.3 us
    all_to_all x1, starting transfers between devices, per_device(): lax.all_to_all(spectra, 'freq', split_axis=2, concat_axis=1, tiled=True)  16.5 us
    dot_general x1, matrix products, per_device(): jnp.einsum('krs,kqs->krq', response[1], gathered[1], preferred_element_ty...  4.2 us
    mul x1, other arithmetic, make_table(): return jnp.concatenate([jnp.cos(phase) * scale, -jnp.sin(phase) * scale], 0)  4.15 us
    all_to_all x1, waiting for transfers between devices, per_device(): lax.all_to_all(spectra, 'freq', split_axis=2, concat_axis=1, tiled=True)  3.18 us
    dot_general x1, matrix products, per_device(): jnp.einsum('krs,kqs->krq', response[1], gathered[0], preferred_element_ty...  2.94 us
  transfers between devices with their start and end apart: 2, of which 2 were waited for; matrix products, arithmetic and copies ran while one was open for 3% of the time, Pallas kernels for 0%

commit v1 on v0

v1 whole, which is shorter than its diff:
```python
import math

import jax
import jax.numpy as jnp
import ml_dtypes
import numpy as np
from jax import lax
from jax.experimental import pallas as pl
from jax.experimental.pallas import tpu as pltpu
from jax.sharding import PartitionSpec as P

NF = 256
NT = 1024
Z = 8

UP = [(y * Z + z, y * Z + (z + 1) % Z) for y in range(2) for z in range(Z)]
DOWN = [(b, a) for a, b in UP]
ACROSS = [(i, (i + Z) % (2 * Z)) for i in range(2 * Z)]

STEPS = [
    [((0, -1), (0, 0), UP), ((0, 1), (0, 0), DOWN), ((1, 0), (0, 0), ACROSS)],
    [((0, -2), (0, -1), UP), ((0, 2), (0, 1), DOWN), ((1, -1), (0, -1), ACROSS)],
    [((0, -3), (0, -2), UP), ((0, 3), (0, 2), DOWN), ((1, 1), (0, 1), ACROSS)],
    [((0, -4), (0, -3), UP), ((1, 2), (1, 1), DOWN), ((1, -2), (0, -2), ACROSS)],
    [((1, -3), (1, -2), UP), ((1, 3), (1, 2), DOWN), ((1, -4), (0, -4), ACROSS)],
]
ORDER = [(0, 0)] + [key for step in STEPS for key, _, _ in step]

KC = 8


def make_table():
    phase = (np.arange(NF)[:, None] * np.arange(NT)[None, :] % NT) * (2.0 * np.pi / NT)
    scale = 1.0 / math.sqrt(NF)
    table = np.concatenate([np.cos(phase) * scale, -np.sin(phase) * scale], 0)
    table = table.reshape(2, NF // 16, 2, KC, NT).transpose(2, 0, 1, 3, 4).reshape(2 * NF, NT)
    high = table.astype(ml_dtypes.bfloat16)
    low = (table - high.astype(np.float64)).astype(ml_dtypes.bfloat16)
    return high, low


def contract_kernel(count, first, last, place_ref, *refs):
    responses, blocks, rest = refs[:count], refs[count : 2 * count], refs[2 * count :]
    out_ref = rest[-1] if not last else rest[-2]
    dims = (((1,), (1,)), ((), ()))
    for k in range(KC):
        total = None if first else rest[0][k]
        for response, block in zip(responses, blocks):
            real, imag = block[0, k], block[1, k]
            for part, right in (
                (response[0, k], jnp.concatenate([real, imag], 0)),
                (response[1, k], jnp.concatenate([-imag, real], 0)),
            ):
                term = lax.dot_general(part, right, dims, preferred_element_type=jnp.float32)
                total = term if total is None else total + term
        if not last:
            out_ref[k] = total
        else:
            rest[-1][k] = total
    if last:
        totals = rest[-1]
        width = totals.shape[2]
        for half in range(out_ref.shape[2] // (2 * width)):

            @pl.when(pl.program_id(0) == half)
            def _():
                for k in range(KC):
                    for parity in range(2):
                        lane = (2 * half + parity) * width
                        out_ref[:, k, lane : lane + width] = totals[k, pl.ds(parity, out_ref.shape[0], stride=2), :]


def contract(response, place, keys, blocks, total, last):
    freqs, recvs, focal = response.shape[1], response.shape[2], blocks[0].shape[2]
    width = blocks[0].shape[3]
    count, first = len(blocks), total is None

    def source(g, at, key):
        column, offset = key
        return 0, g, 0, ((at[0] & Z) ^ (Z * column)) | ((at[0] + (offset % Z)) & (Z - 1))

    in_specs = [
        pl.BlockSpec((2, KC, recvs, width), lambda g, at, key=key: source(g, at, key)) for key in keys
    ] + [pl.BlockSpec((2, KC, focal, width), lambda g, at: (0, g, 0, 0))] * count
    acc_spec = pl.BlockSpec((KC, recvs, 2 * focal), lambda g, at: (g, 0, 0))
    args = [response] * count + list(blocks)
    if not first:
        in_specs.append(acc_spec)
        args.append(total)
    if last:
        shape = (recvs // 2, KC, freqs // KC * 4 * focal)
        out_spec = pl.BlockSpec(shape, lambda g, at: (0, 0, 0))
        scratch = [pltpu.VMEM((KC, recvs, 2 * focal), jnp.float32)]
    else:
        shape = (freqs, recvs, 2 * focal)
        out_spec, scratch = acc_spec, []
    return pl.pallas_call(
        lambda *refs: contract_kernel(count, first, last, *refs),
        out_shape=jax.ShapeDtypeStruct(shape, jnp.float32),
        grid_spec=pltpu.PrefetchScalarGridSpec(
            num_scalar_prefetch=1,
            grid=(freqs // KC,),
            in_specs=in_specs,
            out_specs=out_spec,
            scratch_shapes=scratch,
        ),
        compiler_params=pltpu.CompilerParams(vmem_limit_bytes=16 * 2**20),
        cost_estimate=pl.CostEstimate(
            flops=count * freqs * recvs * focal * width * 8,
            bytes_accessed=count * freqs * (recvs + focal) * width * 4,
            transcendentals=0,
        ),
        name="contract",
    )(place, *args)


def split(x):
    high = x.astype(jnp.bfloat16)
    return high, (x - high.astype(jnp.float32)).astype(jnp.bfloat16)


def transform_kernel(moved_ref, high_ref, low_ref, start_ref, end_ref, out_ref):
    across = moved_ref[...].T
    rows = jnp.concatenate(
        [
            jnp.concatenate(
                [across[64 * half + 32 * parity + 16 * part :][:16] for half in range(2) for part in range(2)], 1
            )
            for parity in range(2)
        ],
        0,
    )
    high, low = split(rows)
    both = jnp.concatenate([high, low], 0)
    dims = (((1,), (0,)), ((), ()))
    width = 256
    for at in range(0, NT, width):
        cols = slice(at, at + width)
        main = lax.dot_general(both, high_ref[:, cols], dims, preferred_element_type=jnp.float32)
        rest = lax.dot_general(high, low_ref[:, cols], dims, preferred_element_type=jnp.float32)
        traces = main[0:32] + (main[32:64] + rest)
        samples = lax.broadcasted_iota(jnp.int32, traces.shape, 1) + at
        keep = (samples >= start_ref[...]) & (samples < end_ref[...])
        traces = jnp.where(keep, traces, 0.0)
        for parity in range(2):
            out_ref[:, parity, cols] = traces[16 * parity : 16 * parity + 16]


def transform(moved, high, low, start, end, focal):
    return pl.pallas_call(
        transform_kernel,
        out_shape=jax.ShapeDtypeStruct((focal, 2, NT), jnp.float32),
        compiler_params=pltpu.CompilerParams(vmem_limit_bytes=16 * 2**20),
        cost_estimate=pl.CostEstimate(flops=32 * 512 * NT * 6, bytes_accessed=2**21, transcendentals=0),
        name="transform",
    )(moved, high, low, start, end)


def per_device(response, focusing, window_onset, window_end):
    focal = focusing.shape[2]
    place = lax.axis_index("recv").astype(jnp.int32).reshape(1)
    blocks = {(0, 0): focusing.astype(jnp.bfloat16)}
    for step in STEPS:
        for key, source, perm in step:
            blocks[key] = lax.ppermute(blocks[source], "recv", perm)
    total = None
    for keys in [ORDER[:1]] + [ORDER[at : at + 3] for at in range(1, 16, 3)]:
        total = contract(response, place, keys, [blocks[key] for key in keys], total, ORDER[-1] in keys)
    moved = lax.all_to_all(total, "freq", split_axis=0, concat_axis=0, tiled=True)
    moved = moved.reshape(-1, moved.shape[2])
    high, low = make_table()
    start = window_onset.T.reshape(2 * focal, 1)
    end = window_end.T.reshape(2 * focal, 1)
    return transform(moved, jnp.asarray(high), jnp.asarray(low), start, end, focal)


def solution(mesh):
    in_specs = (
        P(None, "freq", "recv", None),
        P(None, "freq", None, "recv"),
        P(None, ("recv", "freq")),
        P(None, ("recv", "freq")),
    )
    out_specs = P(None, ("recv", "freq"), None)
    return jax.shard_map(
        per_device, mesh=mesh, in_specs=in_specs, out_specs=out_specs, check_vma=False
    )
```

time: 140 us -> 73.7 us (0.53)
  waiting for transfers between devices: 87.5 us -> 23.9 us
  starting transfers between devices: 16.5 us -> 33.9 us
  between operations: 13.5 us -> 0.13 us
  matrix products: 10.9 us -> 0 us
  Pallas kernels: 0 us -> 10.7 us
  other arithmetic: 6.75 us -> 1.07 us
    all_gather x1 -> x0, waiting for transfers between devices: 84.3 us -> none  [per_device(): gathered = lax.all_gather(focus_half, 'recv', axis=3, tiled=True)]
    ppermute x0 -> x15, starting transfers between devices: none -> 19.6 us  [per_device(): blocks[key] = lax.ppermute(blocks[source], 'recv', perm)]
    ppermute x0 -> x15, waiting for transfers between devices: none -> 16.8 us  [per_device(): blocks[key] = lax.ppermute(blocks[source], 'recv', perm)]
    dot_general x5 -> x0, matrix products: 10.9 us -> none  [the longest x1 4.2 us: per_device(): jnp.einsum('krs,kqs->krq', response[1], gathered[1], preferred_element_ty...]
    pallas_call x0 -> x7, Pallas kernels: none -> 10.7 us  [the longest x6 9.54 us: contract(): pl.pallas_call(lambda *refs: contract_kernel(count, first, last, *refs),...]
    mul x1 -> x0, other arithmetic: 4.15 us -> none  [make_table(): return jnp.concatenate([jnp.cos(phase) * scale, -jnp.sin(phase) * scale], 0)]
    all_to_all x1, waiting for transfers between devices: 3.18 us -> 7.15 us  [per_device(): lax.all_to_all(total, 'freq', split_axis=0, concat_axis=0, tiled=True)]
    all_to_all x1, starting transfers between devices: 16.5 us -> 14.4 us  [per_device(): lax.all_to_all(total, 'freq', split_axis=0, concat_axis=0, tiled=True)]
  transfers between devices with their start and end apart: 2 -> 16, of which waited for: 2 -> 6; matrix products, arithmetic and copies ran while one was open for 3% -> 0% of each run, Pallas kernels for 0% -> 8%
where the time goes in v1:
time: 73.7 us; the launch traced here: 73.4 us
  starting transfers between devices  33.9 us (46%)
  waiting for transfers between devices  23.9 us (32%)
  Pallas kernels  10.7 us (15%)
  local copies, waits for them, and re-layouts  3.57 us (5%)
  other arithmetic  1.07 us (1%)
    ppermute x15, starting transfers between devices, per_device(): blocks[key] = lax.ppermute(blocks[source], 'recv', perm)  19.6 us
    ppermute x15, waiting for transfers between devices, per_device(): blocks[key] = lax.ppermute(blocks[source], 'recv', perm)  16.8 us
    all_to_all x1, starting transfers between devices, per_device(): lax.all_to_all(total, 'freq', split_axis=0, concat_axis=0, tiled=True)  14.4 us
    pallas_call x6, Pallas kernels, contract(): pl.pallas_call(lambda *refs: contract_kernel(count, first, last, *refs),...  9.54 us
    all_to_all x1, waiting for transfers between devices, per_device(): lax.all_to_all(total, 'freq', split_axis=0, concat_axis=0, tiled=True)  7.15 us
    unnamed x10, local copies, waits for them, and re-layouts  3.41 us
  transfers between devices with their start and end apart: 16, of which 6 were waited for; matrix products, arithmetic and copies ran while one was open for 0% of the time, Pallas kernels for 8%

profile of v1, /device:TPU:1, one launch (start us, length us, event | category | flops | bytes accessed | tf_op | source)
XLA Modules:
  0.0 73.4 jit_solution(14632633687021519675)
XLA Ops:
  0.0 1.1 %convert_element_type.3.refs_2_ = bf16[2,16,16,256]{3,2,1,0:T(8,128)(2,1)S(1)} convert(f32[2,16,16,256]{3,2,1,0:T(8,128)} %param.7) | non-fusion elementwise | flops 131072 | bytes 786432 | tf_op jit(solution)/shard_map/convert_element_type | solution.py:162
  1.1 2.5 %collective-permute-start = (bf16[2,16,16,256]{3,2,1,0:T(8,128)(2,1)S(1)}, bf16[2,16,16,256]{3,2,1,0:T(8,128)(2,1)S(1)}, u32[]{:S(2)}, u32[]{:S(2)}) collective-permute-start(bf16[2,16,16,256]{3,2,1,0:T(8,128)(2,1)S(1)} %convert_element_type.3.refs_2_), channel_id=1, source_target_pairs={{0,1},{1,2},{2,3},{3,4},{4,5},{5,6},{6,7},{7,0},{8,9},{9,10},{10,1... | collective-permute-start | bytes 786440 | tf_op jit(solution)/shard_map/ppermute | solution.py:165
  3.6 4.0 %collective-permute-start.4 = (bf16[2,16,16,256]{3,2,1,0:T(8,128)(2,1)S(1)}, bf16[2,16,16,256]{3,2,1,0:T(8,128)(2,1)S(1)}, u32[]{:S(2)}, u32[]{:S(2)}) collective-permute-start(bf16[2,16,16,256]{3,2,1,0:T(8,128)(2,1)S(1)} %convert_element_type.3.refs_2_), channel_id=1, source_target_pairs={{1,0},{2,1},{3,2},{4,3},{5,4},{6,5},{7,6},{0,7},{9,8},{10,9},{11,1... | collective-permute-start | bytes 786440 | tf_op jit(solution)/shard_map/ppermute | solution.py:165
  7.6 5.9 %collective-permute-done.refs_4_ = bf16[2,16,16,256]{3,2,1,0:T(8,128)(2,1)S(1)} collective-permute-done((bf16[2,16,16,256]{3,2,1,0:T(8,128)(2,1)S(1)}, bf16[2,16,16,256]{3,2,1,0:T(8,128)(2,1)S(1)}, u32[]{:S(2)}, u32[]{:S(2)}) %collective-permute-start) | collective-permute-done | bytes 262176 | tf_op jit(solution)/shard_map/ppermute | solution.py:165
  13.6 0.0 collective-permute-start.1
  13.6 0.0 collective-permute-done.4.refs_5_
  13.6 1.3 %collective-permute-start.5 = (bf16[2,16,16,256]{3,2,1,0:T(8,128)(2,1)S(1)}, bf16[2,16,16,256]{3,2,1,0:T(8,128)(2,1)S(1)}, u32[]{:S(2)}, u32[]{:S(2)}) collective-permute-start(bf16[2,16,16,256]{3,2,1,0:T(8,128)(2,1)S(1)} %collective-permute-done.4.refs_5_), channel_id=1, source_target_pairs={{0,8},{1,9},{2,10},{3,11},{4,12},{5,13},{6,14},{7,15},{8,0},{9,1},... | collective-permute-start | bytes 786440 | tf_op jit(solution)/shard_map/ppermute | solution.py:165
  14.9 6.5 %collective-permute-done.1.refs_4_ = bf16[2,16,16,256]{3,2,1,0:T(8,128)(2,1)S(1)} collective-permute-done((bf16[2,16,16,256]{3,2,1,0:T(8,128)(2,1)S(1)}, bf16[2,16,16,256]{3,2,1,0:T(8,128)(2,1)S(1)}, u32[]{:S(2)}, u32[]{:S(2)}) %collective-permute-start.1) | collective-permute-done | bytes 262176 | tf_op jit(solution)/shard_map/ppermute | solution.py:165
  21.4 0.0 collective-permute-start.8
  21.4 1.3 %collective-permute-start.14 = (bf16[2,16,16,256]{3,2,1,0:T(8,128)(2,1)S(1)}, bf16[2,16,16,256]{3,2,1,0:T(8,128)(2,1)S(1)}, u32[]{:S(2)}, u32[]{:S(2)}) collective-permute-start(bf16[2,16,16,256]{3,2,1,0:T(8,128)(2,1)S(1)} %convert_element_type.3.refs_2_), channel_id=1, source_target_pairs={{0,8},{1,9},{2,10},{3,11},{4,12},{5,13},{6,14},{7,15},{8,0},{9,1},... | collective-permute-start | bytes 786440 | tf_op jit(solution)/shard_map/ppermute | solution.py:165
  22.7 2.7 %collective-permute-start.11 = (bf16[2,16,16,256]{3,2,1,0:T(8,128)(2,1)S(1)}, bf16[2,16,16,256]{3,2,1,0:T(8,128)(2,1)S(1)}, u32[]{:S(2)}, u32[]{:S(2)}) collective-permute-start(bf16[2,16,16,256]{3,2,1,0:T(8,128)(2,1)S(1)} %collective-permute-done.4.refs_5_), channel_id=1, source_target_pairs={{1,0},{2,1},{3,2},{4,3},{5,4},{6,5},{7,6},{0,7},{9,8},{10,9},{11,1... | collective-permute-start | bytes 786440 | tf_op jit(solution)/shard_map/ppermute | solution.py:165
  25.3 0.2 collective-permute-start.2
  25.5 0.0 collective-permute-done.5.refs_6_
  25.5 0.0 collective-permute-start.6
  25.5 2.7 %collective-permute-done.8.refs_4_ = bf16[2,16,16,256]{3,2,1,0:T(8,128)(2,1)S(1)} collective-permute-done((bf16[2,16,16,256]{3,2,1,0:T(8,128)(2,1)S(1)}, bf16[2,16,16,256]{3,2,1,0:T(8,128)(2,1)S(1)}, u32[]{:S(2)}, u32[]{:S(2)}) %collective-permute-start.8) | collective-permute-done | bytes 262176 | tf_op jit(solution)/shard_map/ppermute | solution.py:165
  28.2 0.0 collective-permute-start.9
  28.2 0.0 collective-permute-done.14.refs_6_
  28.2 1.3 %collective-permute-start.13 = (bf16[2,16,16,256]{3,2,1,0:T(8,128)(2,1)S(1)}, bf16[2,16,16,256]{3,2,1,0:T(8,128)(2,1)}, u32[]{:S(2)}, u32[]{:S(2)}) collective-permute-start(bf16[2,16,16,256]{3,2,1,0:T(8,128)(2,1)S(1)} %collective-permute-done.refs_4_), channel_id=1, source_target_pairs={{0,8},{1,9},{2,10},{3,11},{4,12},{5,13},{6,14},{7,15},{8,0},{9,1},... | collective-permute-start | bytes 786440 | tf_op jit(solution)/shard_map/ppermute | solution.py:165
  29.5 0.0 collective-permute-done.11.refs_5_
  29.5 2.7 %collective-permute-start.12 = (bf16[2,16,16,256]{3,2,1,0:T(8,128)(2,1)S(1)}, bf16[2,16,16,256]{3,2,1,0:T(8,128)(2,1)}, u32[]{:S(2)}, u32[]{:S(2)}) collective-permute-start(bf16[2,16,16,256]{3,2,1,0:T(8,128)(2,1)S(1)} %collective-permute-done.11.refs_5_), channel_id=1, source_target_pairs={{1,0},{2,1},{3,2},{4,3},{5,4},{6,5},{7,6},{0,7},{9,8},{10,9},{11,1... | collective-permute-start | bytes 786440 | tf_op jit(solution)/shard_map/ppermute | solution.py:165
  32.2 1.2 %collective-permute-done.2.refs_6_ = bf16[2,16,16,256]{3,2,1,0:T(8,128)(2,1)S(1)} collective-permute-done((bf16[2,16,16,256]{3,2,1,0:T(8,128)(2,1)S(1)}, bf16[2,16,16,256]{3,2,1,0:T(8,128)(2,1)S(1)}, u32[]{:S(2)}, u32[]{:S(2)}) %collective-permute-start.2) | collective-permute-done | bytes 262176 | tf_op jit(solution)/shard_map/ppermute | solution.py:165
  33.5 0.0 collective-permute-start.3
  33.5 0.4 collective-permute-done.6.refs_5_
  33.9 3.4 %collective-permute-start.7 = (bf16[2,16,16,256]{3,2,1,0:T(8,128)(2,1)S(1)}, bf16[2,16,16,256]{3,2,1,0:T(8,128)(2,1)S(1)}, u32[]{:S(2)}, u32[]{:S(2)}) collective-permute-start(bf16[2,16,16,256]{3,2,1,0:T(8,128)(2,1)S(1)} %collective-permute-done.6.refs_5_), channel_id=1, source_target_pairs={{1,0},{2,1},{3,2},{4,3},{5,4},{6,5},{7,6},{0,7},{9,8},{10,9},{11,1... | collective-permute-start | bytes 786440 | tf_op jit(solution)/shard_map/ppermute | solution.py:165
  37.3 0.0 collective-permute-done.9.refs_4_
  37.3 0.2 collective-permute-start.10
  37.4 0.0 copy-start
  37.4 3.4 %copy-done = bf16[2,16,32,4096]{3,2,1,0:T(8,128)(2,1)S(1)} copy-done((bf16[2,16,32,4096]{3,2,1,0:T(8,128)(2,1)S(1)}, bf16[2,16,32,4096]{3,2,1,0:T(8,128)(2,1)}, u32[]{:S(2)}) %copy-start) | copy-done | bytes 8388632
  40.8 0.5 contract.6.refs_7_
  41.4 1.1 %contract.7.refs_7_ = f32[16,32,32]{2,1,0:T(8,128)S(1)} custom-call(s32[1]{0:T(128)} %bitcast.refs_0_, bf16[2,16,32,4096]{3,2,1,0:T(8,128)(2,1)S(1)} %copy-done, bf16[2,16,32,4096]{3,2,1,0:T(8,128)(2,1)S(1)} %copy-done, bf16[2,16,32,4096]{3,2,1,0:T(8,128)(2,1)S(1)} %copy-done, bf16[2,16,16,256]{3,2,1,0:T(8,128)(2,1)S(1)} %collective-permute-done.refs_4_, ...), custom_call_target="tpu_custom_call" | custom-call | flops 50331648 | bytes 2359296 | tf_op jit(solution)/shard_map/contract/pallas_call | solution.py:97
  42.4 0.0 collective-permute-done.13.refs_6_
  42.4 1.8 %contract.8.refs_7_ = f32[16,32,32]{2,1,0:T(8,128)S(1)} custom-call(s32[1]{0:T(128)} %bitcast.refs_0_, bf16[2,16,32,4096]{3,2,1,0:T(8,128)(2,1)S(1)} %copy-done, bf16[2,16,32,4096]{3,2,1,0:T(8,128)(2,1)S(1)} %copy-done, bf16[2,16,32,4096]{3,2,1,0:T(8,128)(2,1)S(1)} %copy-done, bf16[2,16,16,256]{3,2,1,0:T(8,128)(2,1)S(1)} %collective-permute-done.1.refs_4_, ...), custom_call_target="tpu_custom_call" | custom-call | flops 50331648 | bytes 2359296 | tf_op jit(solution)/shard_map/contract/pallas_call | solution.py:97
  44.2 0.0 collective-permute-done.12.refs_5_
  44.2 1.8 %contract.9.refs_7_ = f32[16,32,32]{2,1,0:T(8,128)S(1)} custom-call(s32[1]{0:T(128)} %bitcast.refs_0_, bf16[2,16,32,4096]{3,2,1,0:T(8,128)(2,1)S(1)} %copy-done, bf16[2,16,32,4096]{3,2,1,0:T(8,128)(2,1)S(1)} %copy-done, bf16[2,16,32,4096]{3,2,1,0:T(8,128)(2,1)S(1)} %copy-done, bf16[2,16,16,256]{3,2,1,0:T(8,128)(2,1)S(1)} %collective-permute-done.8.refs_4_, ...), custom_call_target="tpu_custom_call" | custom-call | flops 50331648 | bytes 2359296 | tf_op jit(solution)/shard_map/contract/pallas_call | solution.py:97
  46.0 1.0 %contract.10.refs_7_ = f32[16,32,32]{2,1,0:T(8,128)S(1)} custom-call(s32[1]{0:T(128)} %bitcast.refs_0_, bf16[2,16,32,4096]{3,2,1,0:T(8,128)(2,1)S(1)} %copy-done, bf16[2,16,32,4096]{3,2,1,0:T(8,128)(2,1)S(1)} %copy-done, bf16[2,16,32,4096]{3,2,1,0:T(8,128)(2,1)S(1)} %copy-done, bf16[2,16,16,256]{3,2,1,0:T(8,128)(2,1)S(1)} %collective-permute-done.9.refs_4_, ...), custom_call_target="tpu_custom_call" | custom-call | flops 50331648 | bytes 2359296 | tf_op jit(solution)/shard_map/contract/pallas_call | solution.py:97
  47.0 0.0 copy-start.3
  47.1 0.0 copy-start.4
  47.1 0.0 copy-start.1
  47.1 0.0 copy-start.2
  47.1 0.0 collective-permute-done.3.refs_4_
  47.1 0.0 collective-permute-done.7.refs_5_
  47.1 0.0 collective-permute-done.10.refs_6_
  47.1 3.4 %contract.11 = f32[16,8,128]{2,1,0:T(8,128)} custom-call(s32[1]{0:T(128)} %bitcast.refs_0_, bf16[2,16,32,4096]{3,2,1,0:T(8,128)(2,1)S(1)} %copy-done, bf16[2,16,32,4096]{3,2,1,0:T(8,128)(2,1)S(1)} %copy-done, bf16[2,16,32,4096]{3,2,1,0:T(8,128)(2,1)S(1)} %copy-done, bf16[2,16,16,256]{3,2,1,0:T(8,128)(2,1)S(1)} %collective-permute-done.3.refs_4_, ...), custom_call_target="tpu_custom_call" | custom-call | flops 50331648 | bytes 2359296 | tf_op jit(solution)/shard_map/contract/pallas_call | solution.py:97
  50.5 14.4 %all-to-all-start = ((f32[16,8,128]{2,1,0:T(8,128)}), f32[16,8,128]{2,1,0:T(8,128)S(1)}, u32[]{:S(2)}, u32[]{:S(2)}) async-start(f32[16,8,128]{2,1,0:T(8,128)} %contract.11), calls=%async_computation | async-start | bytes 131072 | tf_op jit(solution)/shard_map/all_to_all | solution.py:169
  64.8 0.0 copy-done.3
  64.9 0.1 reshape.16.start_ref
  64.9 0.0 copy-done.4
  64.9 0.1 reshape.17.end_ref
  65.0 7.2 %all-to-all-done = f32[16,8,128]{2,1,0:T(8,128)S(1)} async-done(((f32[16,8,128]{2,1,0:T(8,128)}), f32[16,8,128]{2,1,0:T(8,128)S(1)}, u32[]{:S(2)}, u32[]{:S(2)}) %all-to-all-start) | async-done | bytes 65568 | tf_op jit(solution)/shard_map/all_to_all | solution.py:169
  72.2 0.0 copy-done.1
  72.2 0.0 copy-done.2
  72.2 1.2 %transform.1 = f32[16,2,1024]{2,1,0:T(2,128)} custom-call(f32[128,128]{1,0:T(8,128)S(1)} %bitcast.4, bf16[512,1024]{1,0:T(8,128)(2,1)S(1)} %copy-done.1, bf16[512,1024]{1,0:T(8,128)(2,1)S(1)} %copy-done.2, s32[32,1]{1,0:T(8,128)S(1)} %reshape.16.start_ref, s32[32,1]{1,0:T(8,128)S(1)} %reshape.17.end_ref), custom_call_target="tpu_custom_call" | custom-call | flops 100663296 | bytes 2097152 | tf_op jit(solution)/shard_map/transform/pallas_call | solution.py:150
Async XLA Ops:
  1.1 12.5 %collective-permute-start = (bf16[2,16,16,256]{3,2,1,0:T(8,128)(2,1)S(1)}, bf16[2,16,16,256]{3,2,1,0:T(8,128)(2,1)S(1)}, u32[]{:S(2)}, u32[]{:S(2)}) collective-permute-start(bf16[2,16,16,256]{3,2,1,0:T(8,128)(2,1)S(1)} %convert_element_type.3.refs_2_), channel_id=1, source_target_pairs={{0,1},{1,2},{2,3},{3,4},{4,5},{5,6},{6,7},{7,0},{8,9},{9,10},{10,1... | collective-permute-start | bytes 786440 | tf_op jit(solution)/shard_map/ppermute | solution.py:165
  3.6 10.0 %collective-permute-start.4 = (bf16[2,16,16,256]{3,2,1,0:T(8,128)(2,1)S(1)}, bf16[2,16,16,256]{3,2,1,0:T(8,128)(2,1)S(1)}, u32[]{:S(2)}, u32[]{:S(2)}) collective-permute-start(bf16[2,16,16,256]{3,2,1,0:T(8,128)(2,1)S(1)} %convert_element_type.3.refs_2_), channel_id=1, source_target_pairs={{1,0},{2,1},{3,2},{4,3},{5,4},{6,5},{7,6},{0,7},{9,8},{10,9},{11,1... | collective-permute-start | bytes 786440 | tf_op jit(solution)/shard_map/ppermute | solution.py:165
  13.6 7.8 %collective-permute-start.1 = (bf16[2,16,16,256]{3,2,1,0:T(8,128)(2,1)S(1)}, bf16[2,16,16,256]{3,2,1,0:T(8,128)(2,1)S(1)}, u32[]{:S(2)}, u32[]{:S(2)}) collective-permute-start(bf16[2,16,16,256]{3,2,1,0:T(8,128)(2,1)S(1)} %collective-permute-done.refs_4_), channel_id=1, source_target_pairs={{0,1},{1,2},{2,3},{3,4},{4,5},{5,6},{6,7},{7,0},{8,9},{9,10},{10,1... | collective-permute-start | bytes 786440 | tf_op jit(solution)/shard_map/ppermute | solution.py:165
  13.6 11.9 %collective-permute-start.5 = (bf16[2,16,16,256]{3,2,1,0:T(8,128)(2,1)S(1)}, bf16[2,16,16,256]{3,2,1,0:T(8,128)(2,1)S(1)}, u32[]{:S(2)}, u32[]{:S(2)}) collective-permute-start(bf16[2,16,16,256]{3,2,1,0:T(8,128)(2,1)S(1)} %collective-permute-done.4.refs_5_), channel_id=1, source_target_pairs={{0,8},{1,9},{2,10},{3,11},{4,12},{5,13},{6,14},{7,15},{8,0},{9,1},... | collective-permute-start | bytes 786440 | tf_op jit(solution)/shard_map/ppermute | solution.py:165
  21.4 6.9 %collective-permute-start.8 = (bf16[2,16,16,256]{3,2,1,0:T(8,128)(2,1)S(1)}, bf16[2,16,16,256]{3,2,1,0:T(8,128)(2,1)S(1)}, u32[]{:S(2)}, u32[]{:S(2)}) collective-permute-start(bf16[2,16,16,256]{3,2,1,0:T(8,128)(2,1)S(1)} %collective-permute-done.1.refs_4_), channel_id=1, source_target_pairs={{0,1},{1,2},{2,3},{3,4},{4,5},{5,6},{6,7},{7,0},{8,9},{9,10},{10,1... | collective-permute-start | bytes 786440 | tf_op jit(solution)/shard_map/ppermute | solution.py:165
  21.4 6.9 %collective-permute-start.14 = (bf16[2,16,16,256]{3,2,1,0:T(8,128)(2,1)S(1)}, bf16[2,16,16,256]{3,2,1,0:T(8,128)(2,1)S(1)}, u32[]{:S(2)}, u32[]{:S(2)}) collective-permute-start(bf16[2,16,16,256]{3,2,1,0:T(8,128)(2,1)S(1)} %convert_element_type.3.refs_2_), channel_id=1, source_target_pairs={{0,8},{1,9},{2,10},{3,11},{4,12},{5,13},{6,14},{7,15},{8,0},{9,1},... | collective-permute-start | bytes 786440 | tf_op jit(solution)/shard_map/ppermute | solution.py:165
  22.7 6.9 %collective-permute-start.11 = (bf16[2,16,16,256]{3,2,1,0:T(8,128)(2,1)S(1)}, bf16[2,16,16,256]{3,2,1,0:T(8,128)(2,1)S(1)}, u32[]{:S(2)}, u32[]{:S(2)}) collective-permute-start(bf16[2,16,16,256]{3,2,1,0:T(8,128)(2,1)S(1)} %collective-permute-done.4.refs_5_), channel_id=1, source_target_pairs={{1,0},{2,1},{3,2},{4,3},{5,4},{6,5},{7,6},{0,7},{9,8},{10,9},{11,1... | collective-permute-start | bytes 786440 | tf_op jit(solution)/shard_map/ppermute | solution.py:165
  25.3 8.1 %collective-permute-start.2 = (bf16[2,16,16,256]{3,2,1,0:T(8,128)(2,1)S(1)}, bf16[2,16,16,256]{3,2,1,0:T(8,128)(2,1)S(1)}, u32[]{:S(2)}, u32[]{:S(2)}) collective-permute-start(bf16[2,16,16,256]{3,2,1,0:T(8,128)(2,1)S(1)} %collective-permute-done.1.refs_4_), channel_id=1, source_target_pairs={{0,8},{1,9},{2,10},{3,11},{4,12},{5,13},{6,14},{7,15},{8,0},{9,1},... | collective-permute-start | bytes 786440 | tf_op jit(solution)/shard_map/ppermute | solution.py:165
  25.5 8.3 %collective-permute-start.6 = (bf16[2,16,16,256]{3,2,1,0:T(8,128)(2,1)S(1)}, bf16[2,16,16,256]{3,2,1,0:T(8,128)(2,1)S(1)}, u32[]{:S(2)}, u32[]{:S(2)}) collective-permute-start(bf16[2,16,16,256]{3,2,1,0:T(8,128)(2,1)S(1)} %collective-permute-done.5.refs_6_), channel_id=1, source_target_pairs={{1,0},{2,1},{3,2},{4,3},{5,4},{6,5},{7,6},{0,7},{9,8},{10,9},{11,1... | collective-permute-start | bytes 786440 | tf_op jit(solution)/shard_map/ppermute | solution.py:165
  28.2 9.0 %collective-permute-start.9 = (bf16[2,16,16,256]{3,2,1,0:T(8,128)(2,1)S(1)}, bf16[2,16,16,256]{3,2,1,0:T(8,128)(2,1)S(1)}, u32[]{:S(2)}, u32[]{:S(2)}) collective-permute-start(bf16[2,16,16,256]{3,2,1,0:T(8,128)(2,1)S(1)} %collective-permute-done.8.refs_4_), channel_id=1, source_target_pairs={{0,1},{1,2},{2,3},{3,4},{4,5},{5,6},{6,7},{7,0},{8,9},{9,10},{10,1... | collective-permute-start | bytes 786440 | tf_op jit(solution)/shard_map/ppermute | solution.py:165
  28.2 14.2 %collective-permute-start.13 = (bf16[2,16,16,256]{3,2,1,0:T(8,128)(2,1)S(1)}, bf16[2,16,16,256]{3,2,1,0:T(8,128)(2,1)}, u32[]{:S(2)}, u32[]{:S(2)}) collective-permute-start(bf16[2,16,16,256]{3,2,1,0:T(8,128)(2,1)S(1)} %collective-permute-done.refs_4_), channel_id=1, source_target_pairs={{0,8},{1,9},{2,10},{3,11},{4,12},{5,13},{6,14},{7,15},{8,0},{9,1},... | collective-permute-start | bytes 786440 | tf_op jit(solution)/shard_map/ppermute | solution.py:165
  29.5 14.7 %collective-permute-start.12 = (bf16[2,16,16,256]{3,2,1,0:T(8,128)(2,1)S(1)}, bf16[2,16,16,256]{3,2,1,0:T(8,128)(2,1)}, u32[]{:S(2)}, u32[]{:S(2)}) collective-permute-start(bf16[2,16,16,256]{3,2,1,0:T(8,128)(2,1)S(1)} %collective-permute-done.11.refs_5_), channel_id=1, source_target_pairs={{1,0},{2,1},{3,2},{4,3},{5,4},{6,5},{7,6},{0,7},{9,8},{10,9},{11,1... | collective-permute-start | bytes 786440 | tf_op jit(solution)/shard_map/ppermute | solution.py:165
  33.5 13.6 %collective-permute-start.3 = (bf16[2,16,16,256]{3,2,1,0:T(8,128)(2,1)S(1)}, bf16[2,16,16,256]{3,2,1,0:T(8,128)(2,1)S(1)}, u32[]{:S(2)}, u32[]{:S(2)}) collective-permute-start(bf16[2,16,16,256]{3,2,1,0:T(8,128)(2,1)S(1)} %collective-permute-done.2.refs_6_), channel_id=1, source_target_pairs={{0,1},{1,2},{2,3},{3,4},{4,5},{5,6},{6,7},{7,0},{8,9},{9,10},{10,1... | collective-permute-start | bytes 786440 | tf_op jit(solution)/shard_map/ppermute | solution.py:165
  33.9 13.2 %collective-permute-start.7 = (bf16[2,16,16,256]{3,2,1,0:T(8,128)(2,1)S(1)}, bf16[2,16,16,256]{3,2,1,0:T(8,128)(2,1)S(1)}, u32[]{:S(2)}, u32[]{:S(2)}) collective-permute-start(bf16[2,16,16,256]{3,2,1,0:T(8,128)(2,1)S(1)} %collective-permute-done.6.refs_5_), channel_id=1, source_target_pairs={{1,0},{2,1},{3,2},{4,3},{5,4},{6,5},{7,6},{0,7},{9,8},{10,9},{11,1... | collective-permute-start | bytes 786440 | tf_op jit(solution)/shard_map/ppermute | solution.py:165
  37.3 9.8 %collective-permute-start.10 = (bf16[2,16,16,256]{3,2,1,0:T(8,128)(2,1)S(1)}, bf16[2,16,16,256]{3,2,1,0:T(8,128)(2,1)}, u32[]{:S(2)}, u32[]{:S(2)}) collective-permute-start(bf16[2,16,16,256]{3,2,1,0:T(8,128)(2,1)S(1)} %collective-permute-done.9.refs_4_), channel_id=1, source_target_pairs={{0,8},{1,9},{2,10},{3,11},{4,12},{5,13},{6,14},{7,15},{8,0},{9,1},... | collective-permute-start | bytes 786440 | tf_op jit(solution)/shard_map/ppermute | solution.py:165
  37.4 3.4 %copy-start = (bf16[2,16,32,4096]{3,2,1,0:T(8,128)(2,1)S(1)}, bf16[2,16,32,4096]{3,2,1,0:T(8,128)(2,1)}, u32[]{:S(2)}) copy-start(bf16[2,16,32,4096]{3,2,1,0:T(8,128)(2,1)} %refs_3_.9) | copy-start | bytes 25165828
  47.0 17.8 %copy-start.3 = (s32[16,2]{0,1:T(2,128)S(1)}, s32[16,2]{0,1:T(2,128)}, u32[]{:S(2)}) copy-start(s32[16,2]{0,1:T(2,128)} %param.8) | copy-start | bytes 388
  47.1 17.9 %copy-start.4 = (s32[16,2]{0,1:T(2,128)S(1)}, s32[16,2]{0,1:T(2,128)}, u32[]{:S(2)}) copy-start(s32[16,2]{0,1:T(2,128)} %param.9) | copy-start | bytes 388
  47.1 25.1 %copy-start.1 = (bf16[512,1024]{1,0:T(8,128)(2,1)S(1)}, bf16[512,1024]{1,0:T(8,128)(2,1)}, u32[]{:S(2)}) copy-start(bf16[512,1024]{1,0:T(8,128)(2,1)} %constant.8.clone.high_ref) | copy-start | bytes 3145732
  47.1 25.1 %copy-start.2 = (bf16[512,1024]{1,0:T(8,128)(2,1)S(1)}, bf16[512,1024]{1,0:T(8,128)(2,1)}, u32[]{:S(2)}) copy-start(bf16[512,1024]{1,0:T(8,128)(2,1)} %constant.9.clone.low_ref) | copy-start | bytes 3145732
  50.5 21.7 %all-to-all-start = ((f32[16,8,128]{2,1,0:T(8,128)}), f32[16,8,128]{2,1,0:T(8,128)S(1)}, u32[]{:S(2)}, u32[]{:S(2)}) async-start(f32[16,8,128]{2,1,0:T(8,128)} %contract.11), calls=%async_computation | async-start | bytes 131072 | tf_op jit(solution)/shard_map/all_to_all | solution.py:169

commit v2 on v1

--- a/solution.py
+++ b/solution.py
@@ -19,13 +19,15 @@
 
 STEPS = [
     [((0, -1), (0, 0), UP), ((0, 1), (0, 0), DOWN), ((1, 0), (0, 0), ACROSS)],
-    [((0, -2), (0, -1), UP), ((0, 2), (0, 1), DOWN), ((1, -1), (0, -1), ACROSS)],
-    [((0, -3), (0, -2), UP), ((0, 3), (0, 2), DOWN), ((1, 1), (0, 1), ACROSS)],
-    [((0, -4), (0, -3), UP), ((1, 2), (1, 1), DOWN), ((1, -2), (0, -2), ACROSS)],
+    [((0, -2), (0, -1), UP), ((0, 2), (0, 1), DOWN), ((1, 1), (0, 1), ACROSS)],
+    [((0, -3), (0, -2), UP), ((0, 3), (0, 2), DOWN), ((1, -2), (0, -2), ACROSS)],
+    [((0, -4), (0, -3), UP), ((1, 2), (1, 1), DOWN), ((1, -1), (0, -1), ACROSS)],
     [((1, -3), (1, -2), UP), ((1, 3), (1, 2), DOWN), ((1, -4), (0, -4), ACROSS)],
 ]
-ORDER = [(0, 0)] + [key for step in STEPS for key, _, _ in step]
+LAST = [[send[0] for send in STEPS[3]], [send[0] for send in STEPS[4][:2]], [STEPS[4][2][0]]]
+SENDS = [send for step in STEPS for send in step]
 
+COST = 0.1e9
 KC = 8
 
 
@@ -76,8 +78,8 @@
     count, first = len(blocks), total is None
 
     def source(g, at, key):
-        column, offset = key
-        return 0, g, 0, ((at[0] & Z) ^ (Z * column)) | ((at[0] + (offset % Z)) & (Z - 1))
+        column, distance = key
+        return 0, g, 0, ((at[0] & Z) ^ (Z * column)) | ((at[0] + distance) & (Z - 1))
 
     in_specs = [
         pl.BlockSpec((2, KC, recvs, width), lambda g, at, key=key: source(g, at, key)) for key in keys
@@ -106,7 +108,7 @@
         ),
         compiler_params=pltpu.CompilerParams(vmem_limit_bytes=16 * 2**20),
         cost_estimate=pl.CostEstimate(
-            flops=count * freqs * recvs * focal * width * 8,
+            flops=int(COST * count),
             bytes_accessed=count * freqs * (recvs + focal) * width * 4,
             transcendentals=0,
         ),
@@ -160,12 +162,20 @@
     focal = focusing.shape[2]
     place = lax.axis_index("recv").astype(jnp.int32).reshape(1)
     blocks = {(0, 0): focusing.astype(jnp.bfloat16)}
-    for step in STEPS:
-        for key, source, perm in step:
-            blocks[key] = lax.ppermute(blocks[source], "recv", perm)
-    total = None
-    for keys in [ORDER[:1]] + [ORDER[at : at + 3] for at in range(1, 16, 3)]:
-        total = contract(response, place, keys, [blocks[key] for key in keys], total, ORDER[-1] in keys)
+    total = contract(response, place, [(0, 0)], [blocks[(0, 0)]], None, False)
+    for at, (key, source, perm) in enumerate(SENDS):
+        value = blocks[source]
+        before = SENDS[at - 3][0] if at >= 3 else source
+        if at >= 3 and at % 3 == 0:
+            value, total = lax.optimization_barrier((value, total))
+        if before != source:
+            value, blocks[before] = lax.optimization_barrier((value, blocks[before]))
+        blocks[key] = lax.ppermute(value, "recv", perm)
+        if 5 <= at < 14 and at % 3 == 2:
+            keys = [send[0] for send in STEPS[at // 3 - 1]]
+            total = contract(response, place, keys, [blocks[k] for k in keys], total, False)
+    for keys in LAST:
+        total = contract(response, place, keys, [blocks[k] for k in keys], total, keys is LAST[-1])
     moved = lax.all_to_all(total, "freq", split_axis=0, concat_axis=0, tiled=True)
     moved = moved.reshape(-1, moved.shape[2])
     high, low = make_table()

time: 73.7 us -> 66 us (0.90)
  waiting for transfers between devices: 23.9 us -> 16.8 us
  Pallas kernels: 10.7 us -> 8.27 us
  starting transfers between devices: 33.9 us -> 36 us
    ppermute x15, waiting for transfers between devices: 16.8 us -> 9.65 us  [per_device(): blocks[key] = lax.ppermute(value, 'recv', perm)]
    ppermute x15, starting transfers between devices: 19.6 us -> 23.8 us  [per_device(): blocks[key] = lax.ppermute(value, 'recv', perm)]
    pallas_call x6 -> x7, Pallas kernels: 9.54 us -> 7.07 us  [contract(): pl.pallas_call(lambda *refs: contract_kernel(count, first, last, *refs),...]
    all_to_all x1, starting transfers between devices: 14.4 us -> 12.2 us  [per_device(): lax.all_to_all(total, 'freq', split_axis=0, concat_axis=0, tiled=True)]
  transfers between devices with their start and end apart: 16 -> 16, of which waited for: 6 -> 7; matrix products, arithmetic and copies ran while one was open for 0% -> 0% of each run, Pallas kernels for 8% -> 8%
where the time goes in v2:
time: 66 us; the launch traced here: 65.8 us
  starting transfers between devices  36 us (55%)
  waiting for transfers between devices  16.8 us (25%)
  Pallas kernels  8.27 us (13%)
  local copies, waits for them, and re-layouts  3.57 us (5%)
  other arithmetic  1.07 us (2%)
    ppermute x15, starting transfers between devices, per_device(): blocks[key] = lax.ppermute(value, 'recv', perm)  23.8 us
    all_to_all x1, starting transfers between devices, per_device(): lax.all_to_all(total, 'freq', split_axis=0, concat_axis=0, tiled=True)  12.2 us
    ppermute x15, waiting for transfers between devices, per_device(): blocks[key] = lax.ppermute(value, 'recv', perm)  9.65 us
    all_to_all x1, waiting for transfers between devices, per_device(): lax.all_to_all(total, 'freq', split_axis=0, concat_axis=0, tiled=True)  7.15 us
    pallas_call x7, Pallas kernels, contract(): pl.pallas_call(lambda *refs: contract_kernel(count, first, last, *refs),...  7.07 us
    unnamed x10, local copies, waits for them, and re-layouts  3.41 us
  transfers between devices with their start and end apart: 16, of which 7 were waited for; matrix products, arithmetic and copies ran while one was open for 0% of the time, Pallas kernels for 8%

profile of v2, /device:TPU:1, one launch (start us, length us, event | category | flops | bytes accessed | tf_op | source)
XLA Modules:
  0.0 65.8 jit_solution(154252322076363910)
XLA Ops:
  0.0 1.1 %convert_element_type.3.refs_2_ = bf16[2,16,16,256]{3,2,1,0:T(8,128)(2,1)S(1)} convert(f32[2,16,16,256]{3,2,1,0:T(8,128)} %param.7) | non-fusion elementwise | flops 131072 | bytes 786432 | tf_op jit(solution)/shard_map/convert_element_type | solution.py:164
  1.1 2.5 %collective-permute-start = (bf16[2,16,16,256]{3,2,1,0:T(8,128)(2,1)S(1)}, bf16[2,16,16,256]{3,2,1,0:T(8,128)(2,1)S(1)}, u32[]{:S(2)}, u32[]{:S(2)}) collective-permute-start(bf16[2,16,16,256]{3,2,1,0:T(8,128)(2,1)S(1)} %convert_element_type.3.refs_2_), channel_id=1, source_target_pairs={{0,1},{1,2},{2,3},{3,4},{4,5},{5,6},{6,7},{7,0},{8,9},{9,10},{10,1... | collective-permute-start | bytes 786440 | tf_op jit(solution)/shard_map/ppermute | solution.py:173
  3.6 4.0 %collective-permute-start.2 = (bf16[2,16,16,256]{3,2,1,0:T(8,128)(2,1)S(1)}, bf16[2,16,16,256]{3,2,1,0:T(8,128)(2,1)S(1)}, u32[]{:S(2)}, u32[]{:S(2)}) collective-permute-start(bf16[2,16,16,256]{3,2,1,0:T(8,128)(2,1)S(1)} %convert_element_type.3.refs_2_), channel_id=1, source_target_pairs={{1,0},{2,1},{3,2},{4,3},{5,4},{6,5},{7,6},{0,7},{9,8},{10,9},{11,1... | collective-permute-start | bytes 786440 | tf_op jit(solution)/shard_map/ppermute | solution.py:173
  7.6 1.3 %collective-permute-start.3 = (bf16[2,16,16,256]{3,2,1,0:T(8,128)(2,1)S(1)}, bf16[2,16,16,256]{3,2,1,0:T(8,128)(2,1)S(1)}, u32[]{:S(2)}, u32[]{:S(2)}) collective-permute-start(bf16[2,16,16,256]{3,2,1,0:T(8,128)(2,1)S(1)} %convert_element_type.3.refs_2_), channel_id=1, source_target_pairs={{0,8},{1,9},{2,10},{3,11},{4,12},{5,13},{6,14},{7,15},{8,0},{9,1},... | collective-permute-start | bytes 786440 | tf_op jit(solution)/shard_map/ppermute | solution.py:173
  8.9 0.0 copy-start
  8.9 3.4 %copy-done = bf16[2,16,32,4096]{3,2,1,0:T(8,128)(2,1)S(1)} copy-done((bf16[2,16,32,4096]{3,2,1,0:T(8,128)(2,1)S(1)}, bf16[2,16,32,4096]{3,2,1,0:T(8,128)(2,1)}, u32[]{:S(2)}) %copy-start) | copy-done | bytes 8388632
  12.3 0.5 contract.7.refs_7_
  12.9 0.7 %collective-permute-done.refs_4_ = bf16[2,16,16,256]{3,2,1,0:T(8,128)(2,1)S(1)} collective-permute-done((bf16[2,16,16,256]{3,2,1,0:T(8,128)(2,1)S(1)}, bf16[2,16,16,256]{3,2,1,0:T(8,128)(2,1)S(1)}, u32[]{:S(2)}, u32[]{:S(2)}) %collective-permute-start) | collective-permute-done | bytes 262176 | tf_op jit(solution)/shard_map/ppermute | solution.py:173
  13.6 0.0 collective-permute-start.1
  13.6 0.0 collective-permute-done.2.refs_5_
  13.6 2.7 %collective-permute-start.7 = (bf16[2,16,16,256]{3,2,1,0:T(8,128)(2,1)S(1)}, bf16[2,16,16,256]{3,2,1,0:T(8,128)(2,1)S(1)}, u32[]{:S(2)}, u32[]{:S(2)}) collective-permute-start(bf16[2,16,16,256]{3,2,1,0:T(8,128)(2,1)S(1)} %collective-permute-done.2.refs_5_), channel_id=1, source_target_pairs={{1,0},{2,1},{3,2},{4,3},{5,4},{6,5},{7,6},{0,7},{9,8},{10,9},{11,1... | collective-permute-start | bytes 786440 | tf_op jit(solution)/shard_map/ppermute | solution.py:173
  16.3 0.0 collective-permute-done.3.refs_6_
  16.3 1.3 %collective-permute-start.4 = (bf16[2,16,16,256]{3,2,1,0:T(8,128)(2,1)S(1)}, bf16[2,16,16,256]{3,2,1,0:T(8,128)(2,1)S(1)}, u32[]{:S(2)}, u32[]{:S(2)}) collective-permute-start(bf16[2,16,16,256]{3,2,1,0:T(8,128)(2,1)S(1)} %collective-permute-done.2.refs_5_), channel_id=1, source_target_pairs={{0,8},{1,9},{2,10},{3,11},{4,12},{5,13},{6,14},{7,15},{8,0},{9,1},... | collective-permute-start | bytes 786440 | tf_op jit(solution)/shard_map/ppermute | solution.py:173
  17.6 1.0 %contract.8.refs_7_ = f32[16,32,32]{2,1,0:T(8,128)S(1)} custom-call(s32[1]{0:T(128)} %bitcast.refs_0_, bf16[2,16,32,4096]{3,2,1,0:T(8,128)(2,1)S(1)} %copy-done, bf16[2,16,32,4096]{3,2,1,0:T(8,128)(2,1)S(1)} %copy-done, bf16[2,16,32,4096]{3,2,1,0:T(8,128)(2,1)S(1)} %copy-done, bf16[2,16,16,256]{3,2,1,0:T(8,128)(2,1)S(1)} %collective-permute-done.refs_4_, ...), custom_call_target="tpu_custom_call" | custom-call | flops 300000000 | bytes 2359296 | tf_op jit(solution)/shard_map/contract/pallas_call | solution.py:99
  18.6 2.8 %collective-permute-done.1.refs_4_ = bf16[2,16,16,256]{3,2,1,0:T(8,128)(2,1)S(1)} collective-permute-done((bf16[2,16,16,256]{3,2,1,0:T(8,128)(2,1)S(1)}, bf16[2,16,16,256]{3,2,1,0:T(8,128)(2,1)S(1)}, u32[]{:S(2)}, u32[]{:S(2)}) %collective-permute-start.1) | collective-permute-done | bytes 262176 | tf_op jit(solution)/shard_map/ppermute | solution.py:173
  21.4 0.0 collective-permute-start.6
  21.4 0.0 collective-permute-done.7.refs_5_
  21.4 2.7 %collective-permute-start.8 = (bf16[2,16,16,256]{3,2,1,0:T(8,128)(2,1)S(1)}, bf16[2,16,16,256]{3,2,1,0:T(8,128)(2,1)S(1)}, u32[]{:S(2)}, u32[]{:S(2)}) collective-permute-start(bf16[2,16,16,256]{3,2,1,0:T(8,128)(2,1)S(1)} %collective-permute-done.7.refs_5_), channel_id=1, source_target_pairs={{1,0},{2,1},{3,2},{4,3},{5,4},{6,5},{7,6},{0,7},{9,8},{10,9},{11,1... | collective-permute-start | bytes 786440 | tf_op jit(solution)/shard_map/ppermute | solution.py:173
  24.1 0.0 collective-permute-done.4.refs_6_
  24.1 1.3 %collective-permute-start.5 = (bf16[2,16,16,256]{3,2,1,0:T(8,128)(2,1)S(1)}, bf16[2,16,16,256]{3,2,1,0:T(8,128)(2,1)S(1)}, u32[]{:S(2)}, u32[]{:S(2)}) collective-permute-start(bf16[2,16,16,256]{3,2,1,0:T(8,128)(2,1)S(1)} %collective-permute-done.1.refs_4_), channel_id=1, source_target_pairs={{0,8},{1,9},{2,10},{3,11},{4,12},{5,13},{6,14},{7,15},{8,0},{9,1},... | collective-permute-start | bytes 786440 | tf_op jit(solution)/shard_map/ppermute | solution.py:173
  25.4 1.0 %contract.9.refs_7_ = f32[16,32,32]{2,1,0:T(8,128)S(1)} custom-call(s32[1]{0:T(128)} %bitcast.refs_0_, bf16[2,16,32,4096]{3,2,1,0:T(8,128)(2,1)S(1)} %copy-done, bf16[2,16,32,4096]{3,2,1,0:T(8,128)(2,1)S(1)} %copy-done, bf16[2,16,32,4096]{3,2,1,0:T(8,128)(2,1)S(1)} %copy-done, bf16[2,16,16,256]{3,2,1,0:T(8,128)(2,1)S(1)} %collective-permute-done.1.refs_4_, ...), custom_call_target="tpu_custom_call" | custom-call | flops 300000000 | bytes 2359296 | tf_op jit(solution)/shard_map/contract/pallas_call | solution.py:99
  26.4 1.8 %collective-permute-done.6.refs_4_ = bf16[2,16,16,256]{3,2,1,0:T(8,128)(2,1)S(1)} collective-permute-done((bf16[2,16,16,256]{3,2,1,0:T(8,128)(2,1)S(1)}, bf16[2,16,16,256]{3,2,1,0:T(8,128)(2,1)S(1)}, u32[]{:S(2)}, u32[]{:S(2)}) %collective-permute-start.6) | collective-permute-done | bytes 262176 | tf_op jit(solution)/shard_map/ppermute | solution.py:173
  28.2 0.0 collective-permute-start.9
  28.2 0.0 collective-permute-done.8.refs_5_
  28.2 2.7 %collective-permute-start.13 = (bf16[2,16,16,256]{3,2,1,0:T(8,128)(2,1)S(1)}, bf16[2,16,16,256]{3,2,1,0:T(8,128)(2,1)S(1)}, u32[]{:S(2)}, u32[]{:S(2)}) collective-permute-start(bf16[2,16,16,256]{3,2,1,0:T(8,128)(2,1)S(1)} %collective-permute-done.4.refs_6_), channel_id=1, source_target_pairs={{1,0},{2,1},{3,2},{4,3},{5,4},{6,5},{7,6},{0,7},{9,8},{10,9},{11,1... | collective-permute-start | bytes 786440 | tf_op jit(solution)/shard_map/ppermute | solution.py:173
  30.9 0.0 collective-permute-done.5.refs_6_
  30.9 1.3 %collective-permute-start.10 = (bf16[2,16,16,256]{3,2,1,0:T(8,128)(2,1)S(1)}, bf16[2,16,16,256]{3,2,1,0:T(8,128)(2,1)S(1)}, u32[]{:S(2)}, u32[]{:S(2)}) collective-permute-start(bf16[2,16,16,256]{3,2,1,0:T(8,128)(2,1)S(1)} %collective-permute-done.refs_4_), channel_id=1, source_target_pairs={{0,8},{1,9},{2,10},{3,11},{4,12},{5,13},{6,14},{7,15},{8,0},{9,1},... | collective-permute-start | bytes 786440 | tf_op jit(solution)/shard_map/ppermute | solution.py:173
  32.2 1.0 %contract.10.refs_7_ = f32[16,32,32]{2,1,0:T(8,128)S(1)} custom-call(s32[1]{0:T(128)} %bitcast.refs_0_, bf16[2,16,32,4096]{3,2,1,0:T(8,128)(2,1)S(1)} %copy-done, bf16[2,16,32,4096]{3,2,1,0:T(8,128)(2,1)S(1)} %copy-done, bf16[2,16,32,4096]{3,2,1,0:T(8,128)(2,1)S(1)} %copy-done, bf16[2,16,16,256]{3,2,1,0:T(8,128)(2,1)S(1)} %collective-permute-done.6.refs_4_, ...), custom_call_target="tpu_custom_call" | custom-call | flops 300000000 | bytes 2359296 | tf_op jit(solution)/shard_map/contract/pallas_call | solution.py:99
  33.2 1.4 %collective-permute-done.9.refs_4_ = bf16[2,16,16,256]{3,2,1,0:T(8,128)(2,1)S(1)} collective-permute-done((bf16[2,16,16,256]{3,2,1,0:T(8,128)(2,1)S(1)}, bf16[2,16,16,256]{3,2,1,0:T(8,128)(2,1)S(1)}, u32[]{:S(2)}, u32[]{:S(2)}) %collective-permute-start.9) | collective-permute-done | bytes 262176 | tf_op jit(solution)/shard_map/ppermute | solution.py:173
  34.7 0.0 collective-permute-start.12
  34.7 0.0 collective-permute-done.13.refs_5_
  34.7 2.7 %collective-permute-start.14 = (bf16[2,16,16,256]{3,2,1,0:T(8,128)(2,1)S(1)}, bf16[2,16,16,256]{3,2,1,0:T(8,128)(2,1)S(1)}, u32[]{:S(2)}, u32[]{:S(2)}) collective-permute-start(bf16[2,16,16,256]{3,2,1,0:T(8,128)(2,1)S(1)} %collective-permute-done.13.refs_5_), channel_id=1, source_target_pairs={{1,0},{2,1},{3,2},{4,3},{5,4},{6,5},{7,6},{0,7},{9,8},{10,9},{11,1... | collective-permute-start | bytes 786440 | tf_op jit(solution)/shard_map/ppermute | solution.py:173
  37.3 0.0 collective-permute-done.10.refs_6_
  37.4 1.3 %collective-permute-start.11 = (bf16[2,16,16,256]{3,2,1,0:T(8,128)(2,1)S(1)}, bf16[2,16,16,256]{3,2,1,0:T(8,128)(2,1)S(1)}, u32[]{:S(2)}, u32[]{:S(2)}) collective-permute-start(bf16[2,16,16,256]{3,2,1,0:T(8,128)(2,1)S(1)} %collective-permute-done.9.refs_4_), channel_id=1, source_target_pairs={{0,8},{1,9},{2,10},{3,11},{4,12},{5,13},{6,14},{7,15},{8,0},{9,1},... | collective-permute-start | bytes 786440 | tf_op jit(solution)/shard_map/ppermute | solution.py:173
  38.6 1.0 %contract.11.refs_5_ = f32[16,32,32]{2,1,0:T(8,128)S(1)} custom-call(s32[1]{0:T(128)} %bitcast.refs_0_, bf16[2,16,32,4096]{3,2,1,0:T(8,128)(2,1)S(1)} %copy-done, bf16[2,16,32,4096]{3,2,1,0:T(8,128)(2,1)S(1)} %copy-done, bf16[2,16,32,4096]{3,2,1,0:T(8,128)(2,1)S(1)} %copy-done, bf16[2,16,16,256]{3,2,1,0:T(8,128)(2,1)S(1)} %collective-permute-done.9.refs_4_, ...), custom_call_target="tpu_custom_call" | custom-call | flops 300000000 | bytes 2359296 | tf_op jit(solution)/shard_map/contract/pallas_call | solution.py:99
  39.7 1.4 %collective-permute-done.12.refs_3_ = bf16[2,16,16,256]{3,2,1,0:T(8,128)(2,1)S(1)} collective-permute-done((bf16[2,16,16,256]{3,2,1,0:T(8,128)(2,1)S(1)}, bf16[2,16,16,256]{3,2,1,0:T(8,128)(2,1)S(1)}, u32[]{:S(2)}, u32[]{:S(2)}) %collective-permute-start.12) | collective-permute-done | bytes 262176 | tf_op jit(solution)/shard_map/ppermute | solution.py:173
  41.1 0.0 collective-permute-done.14.refs_4_
  41.1 0.8 %contract.12.refs_3_ = f32[16,32,32]{2,1,0:T(8,128)S(1)} custom-call(s32[1]{0:T(128)} %bitcast.refs_0_, bf16[2,16,32,4096]{3,2,1,0:T(8,128)(2,1)S(1)} %copy-done, bf16[2,16,32,4096]{3,2,1,0:T(8,128)(2,1)S(1)} %copy-done, bf16[2,16,16,256]{3,2,1,0:T(8,128)(2,1)S(1)} %collective-permute-done.12.refs_3_, ...), custom_call_target="tpu_custom_call" | custom-call | flops 200000000 | bytes 1572864 | tf_op jit(solution)/shard_map/contract/pallas_call | solution.py:99
  41.9 0.0 copy-start.3
  41.9 0.0 copy-start.4
  41.9 0.0 copy-start.1
  41.9 0.0 copy-start.2
  41.9 1.4 %collective-permute-done.11.refs_2_ = bf16[2,16,16,256]{3,2,1,0:T(8,128)(2,1)S(1)} collective-permute-done((bf16[2,16,16,256]{3,2,1,0:T(8,128)(2,1)S(1)}, bf16[2,16,16,256]{3,2,1,0:T(8,128)(2,1)S(1)}, u32[]{:S(2)}, u32[]{:S(2)}) %collective-permute-start.11) | collective-permute-done | bytes 262176 | tf_op jit(solution)/shard_map/ppermute | solution.py:173
  43.3 1.7 %contract.13 = f32[16,8,128]{2,1,0:T(8,128)} custom-call(s32[1]{0:T(128)} %bitcast.refs_0_, bf16[2,16,32,4096]{3,2,1,0:T(8,128)(2,1)S(1)} %copy-done, bf16[2,16,16,256]{3,2,1,0:T(8,128)(2,1)S(1)} %collective-permute-done.11.refs_2_, f32[16,32,32]{2,1,0:T(8,128)S(1)} %contract.12.refs_3_), custom_call_target="tpu_custom_call" | custom-call | flops 100000000 | bytes 786432 | tf_op jit(solution)/shard_map/contract/pallas_call | solution.py:99
  45.0 12.2 %all-to-all-start = ((f32[16,8,128]{2,1,0:T(8,128)}), f32[16,8,128]{2,1,0:T(8,128)S(1)}, u32[]{:S(2)}, u32[]{:S(2)}) async-start(f32[16,8,128]{2,1,0:T(8,128)} %contract.13), calls=%async_computation | async-start | bytes 131072 | tf_op jit(solution)/shard_map/all_to_all | solution.py:179
  57.3 0.0 copy-done.3
  57.3 0.1 reshape.16.start_ref
  57.4 0.0 copy-done.4
  57.4 0.1 reshape.17.end_ref
  57.5 7.2 %all-to-all-done = f32[16,8,128]{2,1,0:T(8,128)S(1)} async-done(((f32[16,8,128]{2,1,0:T(8,128)}), f32[16,8,128]{2,1,0:T(8,128)S(1)}, u32[]{:S(2)}, u32[]{:S(2)}) %all-to-all-start) | async-done | bytes 65568 | tf_op jit(solution)/shard_map/all_to_all | solution.py:179
  64.6 0.0 copy-done.1
  64.6 0.0 copy-done.2
  64.6 1.2 %transform.1 = f32[16,2,1024]{2,1,0:T(2,128)} custom-call(f32[128,128]{1,0:T(8,128)S(1)} %bitcast.4, bf16[512,1024]{1,0:T(8,128)(2,1)S(1)} %copy-done.1, bf16[512,1024]{1,0:T(8,128)(2,1)S(1)} %copy-done.2, s32[32,1]{1,0:T(8,128)S(1)} %reshape.16.start_ref, s32[32,1]{1,0:T(8,128)S(1)} %reshape.17.end_ref), custom_call_target="tpu_custom_call" | custom-call | flops 100663296 | bytes 2097152 | tf_op jit(solution)/shard_map/transform/pallas_call | solution.py:152
Async XLA Ops:
  1.1 12.5 %collective-permute-start = (bf16[2,16,16,256]{3,2,1,0:T(8,128)(2,1)S(1)}, bf16[2,16,16,256]{3,2,1,0:T(8,128)(2,1)S(1)}, u32[]{:S(2)}, u32[]{:S(2)}) collective-permute-start(bf16[2,16,16,256]{3,2,1,0:T(8,128)(2,1)S(1)} %convert_element_type.3.refs_2_), channel_id=1, source_target_pairs={{0,1},{1,2},{2,3},{3,4},{4,5},{5,6},{6,7},{7,0},{8,9},{9,10},{10,1... | collective-permute-start | bytes 786440 | tf_op jit(solution)/shard_map/ppermute | solution.py:173
  3.6 10.0 %collective-permute-start.2 = (bf16[2,16,16,256]{3,2,1,0:T(8,128)(2,1)S(1)}, bf16[2,16,16,256]{3,2,1,0:T(8,128)(2,1)S(1)}, u32[]{:S(2)}, u32[]{:S(2)}) collective-permute-start(bf16[2,16,16,256]{3,2,1,0:T(8,128)(2,1)S(1)} %convert_element_type.3.refs_2_), channel_id=1, source_target_pairs={{1,0},{2,1},{3,2},{4,3},{5,4},{6,5},{7,6},{0,7},{9,8},{10,9},{11,1... | collective-permute-start | bytes 786440 | tf_op jit(solution)/shard_map/ppermute | solution.py:173
  7.6 8.6 %collective-permute-start.3 = (bf16[2,16,16,256]{3,2,1,0:T(8,128)(2,1)S(1)}, bf16[2,16,16,256]{3,2,1,0:T(8,128)(2,1)S(1)}, u32[]{:S(2)}, u32[]{:S(2)}) collective-permute-start(bf16[2,16,16,256]{3,2,1,0:T(8,128)(2,1)S(1)} %convert_element_type.3.refs_2_), channel_id=1, source_target_pairs={{0,8},{1,9},{2,10},{3,11},{4,12},{5,13},{6,14},{7,15},{8,0},{9,1},... | collective-permute-start | bytes 786440 | tf_op jit(solution)/shard_map/ppermute | solution.py:173
  8.9 3.4 %copy-start = (bf16[2,16,32,4096]{3,2,1,0:T(8,128)(2,1)S(1)}, bf16[2,16,32,4096]{3,2,1,0:T(8,128)(2,1)}, u32[]{:S(2)}) copy-start(bf16[2,16,32,4096]{3,2,1,0:T(8,128)(2,1)} %refs_1_.13) | copy-start | bytes 25165828
  13.6 7.8 %collective-permute-start.1 = (bf16[2,16,16,256]{3,2,1,0:T(8,128)(2,1)S(1)}, bf16[2,16,16,256]{3,2,1,0:T(8,128)(2,1)S(1)}, u32[]{:S(2)}, u32[]{:S(2)}) collective-permute-start(bf16[2,16,16,256]{3,2,1,0:T(8,128)(2,1)S(1)} %collective-permute-done.refs_4_), channel_id=1, source_target_pairs={{0,1},{1,2},{2,3},{3,4},{4,5},{5,6},{6,7},{7,0},{8,9},{9,10},{10,1... | collective-permute-start | bytes 786440 | tf_op jit(solution)/shard_map/ppermute | solution.py:173
  13.6 7.8 %collective-permute-start.7 = (bf16[2,16,16,256]{3,2,1,0:T(8,128)(2,1)S(1)}, bf16[2,16,16,256]{3,2,1,0:T(8,128)(2,1)S(1)}, u32[]{:S(2)}, u32[]{:S(2)}) collective-permute-start(bf16[2,16,16,256]{3,2,1,0:T(8,128)(2,1)S(1)} %collective-permute-done.2.refs_5_), channel_id=1, source_target_pairs={{1,0},{2,1},{3,2},{4,3},{5,4},{6,5},{7,6},{0,7},{9,8},{10,9},{11,1... | collective-permute-start | bytes 786440 | tf_op jit(solution)/shard_map/ppermute | solution.py:173
  16.3 7.8 %collective-permute-start.4 = (bf16[2,16,16,256]{3,2,1,0:T(8,128)(2,1)S(1)}, bf16[2,16,16,256]{3,2,1,0:T(8,128)(2,1)S(1)}, u32[]{:S(2)}, u32[]{:S(2)}) collective-permute-start(bf16[2,16,16,256]{3,2,1,0:T(8,128)(2,1)S(1)} %collective-permute-done.2.refs_5_), channel_id=1, source_target_pairs={{0,8},{1,9},{2,10},{3,11},{4,12},{5,13},{6,14},{7,15},{8,0},{9,1},... | collective-permute-start | bytes 786440 | tf_op jit(solution)/shard_map/ppermute | solution.py:173
  21.4 6.9 %collective-permute-start.6 = (bf16[2,16,16,256]{3,2,1,0:T(8,128)(2,1)S(1)}, bf16[2,16,16,256]{3,2,1,0:T(8,128)(2,1)S(1)}, u32[]{:S(2)}, u32[]{:S(2)}) collective-permute-start(bf16[2,16,16,256]{3,2,1,0:T(8,128)(2,1)S(1)} %collective-permute-done.1.refs_4_), channel_id=1, source_target_pairs={{0,1},{1,2},{2,3},{3,4},{4,5},{5,6},{6,7},{7,0},{8,9},{9,10},{10,1... | collective-permute-start | bytes 786440 | tf_op jit(solution)/shard_map/ppermute | solution.py:173
  21.4 6.9 %collective-permute-start.8 = (bf16[2,16,16,256]{3,2,1,0:T(8,128)(2,1)S(1)}, bf16[2,16,16,256]{3,2,1,0:T(8,128)(2,1)S(1)}, u32[]{:S(2)}, u32[]{:S(2)}) collective-permute-start(bf16[2,16,16,256]{3,2,1,0:T(8,128)(2,1)S(1)} %collective-permute-done.7.refs_5_), channel_id=1, source_target_pairs={{1,0},{2,1},{3,2},{4,3},{5,4},{6,5},{7,6},{0,7},{9,8},{10,9},{11,1... | collective-permute-start | bytes 786440 | tf_op jit(solution)/shard_map/ppermute | solution.py:173
  24.1 6.9 %collective-permute-start.5 = (bf16[2,16,16,256]{3,2,1,0:T(8,128)(2,1)S(1)}, bf16[2,16,16,256]{3,2,1,0:T(8,128)(2,1)S(1)}, u32[]{:S(2)}, u32[]{:S(2)}) collective-permute-start(bf16[2,16,16,256]{3,2,1,0:T(8,128)(2,1)S(1)} %collective-permute-done.1.refs_4_), channel_id=1, source_target_pairs={{0,8},{1,9},{2,10},{3,11},{4,12},{5,13},{6,14},{7,15},{8,0},{9,1},... | collective-permute-start | bytes 786440 | tf_op jit(solution)/shard_map/ppermute | solution.py:173
  28.2 6.4 %collective-permute-start.9 = (bf16[2,16,16,256]{3,2,1,0:T(8,128)(2,1)S(1)}, bf16[2,16,16,256]{3,2,1,0:T(8,128)(2,1)S(1)}, u32[]{:S(2)}, u32[]{:S(2)}) collective-permute-start(bf16[2,16,16,256]{3,2,1,0:T(8,128)(2,1)S(1)} %collective-permute-done.6.refs_4_), channel_id=1, source_target_pairs={{0,1},{1,2},{2,3},{3,4},{4,5},{5,6},{6,7},{7,0},{8,9},{9,10},{10,1... | collective-permute-start | bytes 786440 | tf_op jit(solution)/shard_map/ppermute | solution.py:173
  28.2 6.4 %collective-permute-start.13 = (bf16[2,16,16,256]{3,2,1,0:T(8,128)(2,1)S(1)}, bf16[2,16,16,256]{3,2,1,0:T(8,128)(2,1)S(1)}, u32[]{:S(2)}, u32[]{:S(2)}) collective-permute-start(bf16[2,16,16,256]{3,2,1,0:T(8,128)(2,1)S(1)} %collective-permute-done.4.refs_6_), channel_id=1, source_target_pairs={{1,0},{2,1},{3,2},{4,3},{5,4},{6,5},{7,6},{0,7},{9,8},{10,9},{11,1... | collective-permute-start | bytes 786440 | tf_op jit(solution)/shard_map/ppermute | solution.py:173
  30.9 6.4 %collective-permute-start.10 = (bf16[2,16,16,256]{3,2,1,0:T(8,128)(2,1)S(1)}, bf16[2,16,16,256]{3,2,1,0:T(8,128)(2,1)S(1)}, u32[]{:S(2)}, u32[]{:S(2)}) collective-permute-start(bf16[2,16,16,256]{3,2,1,0:T(8,128)(2,1)S(1)} %collective-permute-done.refs_4_), channel_id=1, source_target_pairs={{0,8},{1,9},{2,10},{3,11},{4,12},{5,13},{6,14},{7,15},{8,0},{9,1},... | collective-permute-start | bytes 786440 | tf_op jit(solution)/shard_map/ppermute | solution.py:173
  34.7 6.4 %collective-permute-start.12 = (bf16[2,16,16,256]{3,2,1,0:T(8,128)(2,1)S(1)}, bf16[2,16,16,256]{3,2,1,0:T(8,128)(2,1)S(1)}, u32[]{:S(2)}, u32[]{:S(2)}) collective-permute-start(bf16[2,16,16,256]{3,2,1,0:T(8,128)(2,1)S(1)} %collective-permute-done.5.refs_6_), channel_id=1, source_target_pairs={{0,1},{1,2},{2,3},{3,4},{4,5},{5,6},{6,7},{7,0},{8,9},{9,10},{10,1... | collective-permute-start | bytes 786440 | tf_op jit(solution)/shard_map/ppermute | solution.py:173
  34.7 6.4 %collective-permute-start.14 = (bf16[2,16,16,256]{3,2,1,0:T(8,128)(2,1)S(1)}, bf16[2,16,16,256]{3,2,1,0:T(8,128)(2,1)S(1)}, u32[]{:S(2)}, u32[]{:S(2)}) collective-permute-start(bf16[2,16,16,256]{3,2,1,0:T(8,128)(2,1)S(1)} %collective-permute-done.13.refs_5_), channel_id=1, source_target_pairs={{1,0},{2,1},{3,2},{4,3},{5,4},{6,5},{7,6},{0,7},{9,8},{10,9},{11,1... | collective-permute-start | bytes 786440 | tf_op jit(solution)/shard_map/ppermute | solution.py:173
  37.4 6.0 %collective-permute-start.11 = (bf16[2,16,16,256]{3,2,1,0:T(8,128)(2,1)S(1)}, bf16[2,16,16,256]{3,2,1,0:T(8,128)(2,1)S(1)}, u32[]{:S(2)}, u32[]{:S(2)}) collective-permute-start(bf16[2,16,16,256]{3,2,1,0:T(8,128)(2,1)S(1)} %collective-permute-done.9.refs_4_), channel_id=1, source_target_pairs={{0,8},{1,9},{2,10},{3,11},{4,12},{5,13},{6,14},{7,15},{8,0},{9,1},... | collective-permute-start | bytes 786440 | tf_op jit(solution)/shard_map/ppermute | solution.py:173
  41.9 15.4 %copy-start.3 = (s32[16,2]{0,1:T(2,128)S(1)}, s32[16,2]{0,1:T(2,128)}, u32[]{:S(2)}) copy-start(s32[16,2]{0,1:T(2,128)} %param.8) | copy-start | bytes 388
  41.9 15.5 %copy-start.4 = (s32[16,2]{0,1:T(2,128)S(1)}, s32[16,2]{0,1:T(2,128)}, u32[]{:S(2)}) copy-start(s32[16,2]{0,1:T(2,128)} %param.9) | copy-start | bytes 388
  41.9 22.7 %copy-start.1 = (bf16[512,1024]{1,0:T(8,128)(2,1)S(1)}, bf16[512,1024]{1,0:T(8,128)(2,1)}, u32[]{:S(2)}) copy-start(bf16[512,1024]{1,0:T(8,128)(2,1)} %constant.8.clone.high_ref) | copy-start | bytes 3145732
  41.9 22.7 %copy-start.2 = (bf16[512,1024]{1,0:T(8,128)(2,1)S(1)}, bf16[512,1024]{1,0:T(8,128)(2,1)}, u32[]{:S(2)}) copy-start(bf16[512,1024]{1,0:T(8,128)(2,1)} %constant.9.clone.low_ref) | copy-start | bytes 3145732
  45.0 19.6 %all-to-all-start = ((f32[16,8,128]{2,1,0:T(8,128)}), f32[16,8,128]{2,1,0:T(8,128)S(1)}, u32[]{:S(2)}, u32[]{:S(2)}) async-start(f32[16,8,128]{2,1,0:T(8,128)} %contract.13), calls=%async_computation | async-start | bytes 131072 | tf_op jit(solution)/shard_map/all_to_all | solution.py:179

commit v3 on v2

--- a/solution.py
+++ b/solution.py
@@ -41,11 +41,11 @@
     return high, low
 
 
-def contract_kernel(count, first, last, place_ref, *refs):
+def contract_kernel(count, chunk, first, last, place_ref, *refs):
     responses, blocks, rest = refs[:count], refs[count : 2 * count], refs[2 * count :]
     out_ref = rest[-1] if not last else rest[-2]
     dims = (((1,), (1,)), ((), ()))
-    for k in range(KC):
+    for k in range(chunk):
         total = None if first else rest[0][k]
         for response, block in zip(responses, blocks):
             real, imag = block[0, k], block[1, k]
@@ -62,29 +62,28 @@
     if last:
         totals = rest[-1]
         width = totals.shape[2]
-        for half in range(out_ref.shape[2] // (2 * width)):
-
-            @pl.when(pl.program_id(0) == half)
-            def _():
-                for k in range(KC):
-                    for parity in range(2):
-                        lane = (2 * half + parity) * width
-                        out_ref[:, k, lane : lane + width] = totals[k, pl.ds(parity, out_ref.shape[0], stride=2), :]
+        for half in range(chunk // KC):
+            for k in range(KC):
+                for parity in range(2):
+                    lane = (2 * half + parity) * width
+                    rows = totals[half * KC + k, pl.ds(parity, out_ref.shape[0], stride=2), :]
+                    out_ref[:, k, lane : lane + width] = rows
 
 
 def contract(response, place, keys, blocks, total, last):
     freqs, recvs, focal = response.shape[1], response.shape[2], blocks[0].shape[2]
     width = blocks[0].shape[3]
     count, first = len(blocks), total is None
+    chunk = freqs
 
     def source(g, at, key):
         column, distance = key
         return 0, g, 0, ((at[0] & Z) ^ (Z * column)) | ((at[0] + distance) & (Z - 1))
 
     in_specs = [
-        pl.BlockSpec((2, KC, recvs, width), lambda g, at, key=key: source(g, at, key)) for key in keys
-    ] + [pl.BlockSpec((2, KC, focal, width), lambda g, at: (0, g, 0, 0))] * count
-    acc_spec = pl.BlockSpec((KC, recvs, 2 * focal), lambda g, at: (g, 0, 0))
+        pl.BlockSpec((2, chunk, recvs, width), lambda g, at, key=key: source(g, at, key)) for key in keys
+    ] + [pl.BlockSpec((2, chunk, focal, width), lambda g, at: (0, g, 0, 0))] * count
+    acc_spec = pl.BlockSpec((chunk, recvs, 2 * focal), lambda g, at: (g, 0, 0))
     args = [response] * count + list(blocks)
     if not first:
         in_specs.append(acc_spec)
@@ -92,16 +91,16 @@
     if last:
         shape = (recvs // 2, KC, freqs // KC * 4 * focal)
         out_spec = pl.BlockSpec(shape, lambda g, at: (0, 0, 0))
-        scratch = [pltpu.VMEM((KC, recvs, 2 * focal), jnp.float32)]
+        scratch = [pltpu.VMEM((chunk, recvs, 2 * focal), jnp.float32)]
     else:
         shape = (freqs, recvs, 2 * focal)
         out_spec, scratch = acc_spec, []
     return pl.pallas_call(
-        lambda *refs: contract_kernel(count, first, last, *refs),
+        lambda *refs: contract_kernel(count, chunk, first, last, *refs),
         out_shape=jax.ShapeDtypeStruct(shape, jnp.float32),
         grid_spec=pltpu.PrefetchScalarGridSpec(
             num_scalar_prefetch=1,
-            grid=(freqs // KC,),
+            grid=(freqs // chunk,),
             in_specs=in_specs,
             out_specs=out_spec,
             scratch_shapes=scratch,

time: 66 us -> 65.6 us (level)
  Pallas kernels: 8.27 us -> 5.37 us
  waiting for transfers between devices: 16.8 us -> 19.3 us
    pallas_call x7, Pallas kernels: 7.07 us -> 4.17 us  [contract(): pl.pallas_call(lambda *refs: contract_kernel(count, chunk, first, last, *...]
    ppermute x15, waiting for transfers between devices: 9.65 us -> 12.2 us  [per_device(): blocks[key] = lax.ppermute(value, 'recv', perm)]
  transfers between devices with their start and end apart: 16 -> 16, of which waited for: 7 -> 7; matrix products, arithmetic and copies ran while one was open for 0% -> 0% of each run, Pallas kernels for 8% -> 4%
where the time goes in v3:
time: 65.6 us; the launch traced here: 65.4 us
  starting transfers between devices  36 us (55%)
  waiting for transfers between devices  19.3 us (29%)
  Pallas kernels  5.37 us (8%)
  local copies, waits for them, and re-layouts  3.56 us (5%)
  other arithmetic  1.07 us (2%)
    ppermute x15, starting transfers between devices, per_device(): blocks[key] = lax.ppermute(value, 'recv', perm)  23.8 us
    all_to_all x1, starting transfers between devices, per_device(): lax.all_to_all(total, 'freq', split_axis=0, concat_axis=0, tiled=True)  12.2 us
    ppermute x15, waiting for transfers between devices, per_device(): blocks[key] = lax.ppermute(value, 'recv', perm)  12.2 us
    all_to_all x1, waiting for transfers between devices, per_device(): lax.all_to_all(total, 'freq', split_axis=0, concat_axis=0, tiled=True)  7.15 us
    pallas_call x7, Pallas kernels, contract(): pl.pallas_call(lambda *refs: contract_kernel(count, chunk, first, last, *...  4.17 us
    unnamed x10, local copies, waits for them, and re-layouts  3.4 us
  transfers between devices with their start and end apart: 16, of which 7 were waited for; matrix products, arithmetic and copies ran while one was open for 0% of the time, Pallas kernels for 4%

profile of v3, /device:TPU:1, one launch (start us, length us, event | category | flops | bytes accessed | tf_op | source)
XLA Modules:
  0.0 65.4 jit_solution(15662488525592567020)
XLA Ops:
  0.0 1.1 %convert_element_type.3.refs_2_ = bf16[2,16,16,256]{3,2,1,0:T(8,128)(2,1)S(1)} convert(f32[2,16,16,256]{3,2,1,0:T(8,128)} %param.7) | non-fusion elementwise | flops 131072 | bytes 786432 | tf_op jit(solution)/shard_map/convert_element_type | solution.py:163
  1.1 2.5 %collective-permute-start = (bf16[2,16,16,256]{3,2,1,0:T(8,128)(2,1)S(1)}, bf16[2,16,16,256]{3,2,1,0:T(8,128)(2,1)S(1)}, u32[]{:S(2)}, u32[]{:S(2)}) collective-permute-start(bf16[2,16,16,256]{3,2,1,0:T(8,128)(2,1)S(1)} %convert_element_type.3.refs_2_), channel_id=1, source_target_pairs={{0,1},{1,2},{2,3},{3,4},{4,5},{5,6},{6,7},{7,0},{8,9},{9,10},{10,1... | collective-permute-start | bytes 786440 | tf_op jit(solution)/shard_map/ppermute | solution.py:172
  3.6 4.0 %collective-permute-start.2 = (bf16[2,16,16,256]{3,2,1,0:T(8,128)(2,1)S(1)}, bf16[2,16,16,256]{3,2,1,0:T(8,128)(2,1)S(1)}, u32[]{:S(2)}, u32[]{:S(2)}) collective-permute-start(bf16[2,16,16,256]{3,2,1,0:T(8,128)(2,1)S(1)} %convert_element_type.3.refs_2_), channel_id=1, source_target_pairs={{1,0},{2,1},{3,2},{4,3},{5,4},{6,5},{7,6},{0,7},{9,8},{10,9},{11,1... | collective-permute-start | bytes 786440 | tf_op jit(solution)/shard_map/ppermute | solution.py:172
  7.6 1.3 %collective-permute-start.3 = (bf16[2,16,16,256]{3,2,1,0:T(8,128)(2,1)S(1)}, bf16[2,16,16,256]{3,2,1,0:T(8,128)(2,1)S(1)}, u32[]{:S(2)}, u32[]{:S(2)}) collective-permute-start(bf16[2,16,16,256]{3,2,1,0:T(8,128)(2,1)S(1)} %convert_element_type.3.refs_2_), channel_id=1, source_target_pairs={{0,8},{1,9},{2,10},{3,11},{4,12},{5,13},{6,14},{7,15},{8,0},{9,1},... | collective-permute-start | bytes 786440 | tf_op jit(solution)/shard_map/ppermute | solution.py:172
  8.9 0.0 copy-start
  8.9 3.4 %copy-done = bf16[2,16,32,4096]{3,2,1,0:T(8,128)(2,1)S(1)} copy-done((bf16[2,16,32,4096]{3,2,1,0:T(8,128)(2,1)S(1)}, bf16[2,16,32,4096]{3,2,1,0:T(8,128)(2,1)}, u32[]{:S(2)}) %copy-start) | copy-done | bytes 8388632
  12.3 0.3 contract.7.refs_7_
  12.6 1.0 %collective-permute-done.refs_4_ = bf16[2,16,16,256]{3,2,1,0:T(8,128)(2,1)S(1)} collective-permute-done((bf16[2,16,16,256]{3,2,1,0:T(8,128)(2,1)S(1)}, bf16[2,16,16,256]{3,2,1,0:T(8,128)(2,1)S(1)}, u32[]{:S(2)}, u32[]{:S(2)}) %collective-permute-start) | collective-permute-done | bytes 262176 | tf_op jit(solution)/shard_map/ppermute | solution.py:172
  13.6 0.0 collective-permute-start.1
  13.6 0.0 collective-permute-done.2.refs_5_
  13.6 2.7 %collective-permute-start.7 = (bf16[2,16,16,256]{3,2,1,0:T(8,128)(2,1)S(1)}, bf16[2,16,16,256]{3,2,1,0:T(8,128)(2,1)S(1)}, u32[]{:S(2)}, u32[]{:S(2)}) collective-permute-start(bf16[2,16,16,256]{3,2,1,0:T(8,128)(2,1)S(1)} %collective-permute-done.2.refs_5_), channel_id=1, source_target_pairs={{1,0},{2,1},{3,2},{4,3},{5,4},{6,5},{7,6},{0,7},{9,8},{10,9},{11,1... | collective-permute-start | bytes 786440 | tf_op jit(solution)/shard_map/ppermute | solution.py:172
  16.3 0.0 collective-permute-done.3.refs_6_
  16.3 1.3 %collective-permute-start.4 = (bf16[2,16,16,256]{3,2,1,0:T(8,128)(2,1)S(1)}, bf16[2,16,16,256]{3,2,1,0:T(8,128)(2,1)S(1)}, u32[]{:S(2)}, u32[]{:S(2)}) collective-permute-start(bf16[2,16,16,256]{3,2,1,0:T(8,128)(2,1)S(1)} %collective-permute-done.2.refs_5_), channel_id=1, source_target_pairs={{0,8},{1,9},{2,10},{3,11},{4,12},{5,13},{6,14},{7,15},{8,0},{9,1},... | collective-permute-start | bytes 786440 | tf_op jit(solution)/shard_map/ppermute | solution.py:172
  17.6 0.6 contract.8.refs_7_
  18.1 3.2 %collective-permute-done.1.refs_4_ = bf16[2,16,16,256]{3,2,1,0:T(8,128)(2,1)S(1)} collective-permute-done((bf16[2,16,16,256]{3,2,1,0:T(8,128)(2,1)S(1)}, bf16[2,16,16,256]{3,2,1,0:T(8,128)(2,1)S(1)}, u32[]{:S(2)}, u32[]{:S(2)}) %collective-permute-start.1) | collective-permute-done | bytes 262176 | tf_op jit(solution)/shard_map/ppermute | solution.py:172
  21.4 0.0 collective-permute-start.6
  21.4 0.0 collective-permute-done.7.refs_5_
  21.4 2.7 %collective-permute-start.8 = (bf16[2,16,16,256]{3,2,1,0:T(8,128)(2,1)S(1)}, bf16[2,16,16,256]{3,2,1,0:T(8,128)(2,1)S(1)}, u32[]{:S(2)}, u32[]{:S(2)}) collective-permute-start(bf16[2,16,16,256]{3,2,1,0:T(8,128)(2,1)S(1)} %collective-permute-done.7.refs_5_), channel_id=1, source_target_pairs={{1,0},{2,1},{3,2},{4,3},{5,4},{6,5},{7,6},{0,7},{9,8},{10,9},{11,1... | collective-permute-start | bytes 786440 | tf_op jit(solution)/shard_map/ppermute | solution.py:172
  24.1 0.0 collective-permute-done.4.refs_6_
  24.1 1.3 %collective-permute-start.5 = (bf16[2,16,16,256]{3,2,1,0:T(8,128)(2,1)S(1)}, bf16[2,16,16,256]{3,2,1,0:T(8,128)(2,1)S(1)}, u32[]{:S(2)}, u32[]{:S(2)}) collective-permute-start(bf16[2,16,16,256]{3,2,1,0:T(8,128)(2,1)S(1)} %collective-permute-done.1.refs_4_), channel_id=1, source_target_pairs={{0,8},{1,9},{2,10},{3,11},{4,12},{5,13},{6,14},{7,15},{8,0},{9,1},... | collective-permute-start | bytes 786440 | tf_op jit(solution)/shard_map/ppermute | solution.py:172
  25.4 0.6 contract.9.refs_7_
  25.9 2.3 %collective-permute-done.6.refs_4_ = bf16[2,16,16,256]{3,2,1,0:T(8,128)(2,1)S(1)} collective-permute-done((bf16[2,16,16,256]{3,2,1,0:T(8,128)(2,1)S(1)}, bf16[2,16,16,256]{3,2,1,0:T(8,128)(2,1)S(1)}, u32[]{:S(2)}, u32[]{:S(2)}) %collective-permute-start.6) | collective-permute-done | bytes 262176 | tf_op jit(solution)/shard_map/ppermute | solution.py:172
  28.2 0.0 collective-permute-start.9
  28.2 0.0 collective-permute-done.8.refs_5_
  28.2 2.7 %collective-permute-start.13 = (bf16[2,16,16,256]{3,2,1,0:T(8,128)(2,1)S(1)}, bf16[2,16,16,256]{3,2,1,0:T(8,128)(2,1)S(1)}, u32[]{:S(2)}, u32[]{:S(2)}) collective-permute-start(bf16[2,16,16,256]{3,2,1,0:T(8,128)(2,1)S(1)} %collective-permute-done.4.refs_6_), channel_id=1, source_target_pairs={{1,0},{2,1},{3,2},{4,3},{5,4},{6,5},{7,6},{0,7},{9,8},{10,9},{11,1... | collective-permute-start | bytes 786440 | tf_op jit(solution)/shard_map/ppermute | solution.py:172
  30.9 0.0 collective-permute-done.5.refs_6_
  30.9 1.3 %collective-permute-start.10 = (bf16[2,16,16,256]{3,2,1,0:T(8,128)(2,1)S(1)}, bf16[2,16,16,256]{3,2,1,0:T(8,128)(2,1)S(1)}, u32[]{:S(2)}, u32[]{:S(2)}) collective-permute-start(bf16[2,16,16,256]{3,2,1,0:T(8,128)(2,1)S(1)} %collective-permute-done.refs_4_), channel_id=1, source_target_pairs={{0,8},{1,9},{2,10},{3,11},{4,12},{5,13},{6,14},{7,15},{8,0},{9,1},... | collective-permute-start | bytes 786440 | tf_op jit(solution)/shard_map/ppermute | solution.py:172
  32.2 0.5 contract.10.refs_7_
  32.8 1.9 %collective-permute-done.9.refs_4_ = bf16[2,16,16,256]{3,2,1,0:T(8,128)(2,1)S(1)} collective-permute-done((bf16[2,16,16,256]{3,2,1,0:T(8,128)(2,1)S(1)}, bf16[2,16,16,256]{3,2,1,0:T(8,128)(2,1)S(1)}, u32[]{:S(2)}, u32[]{:S(2)}) %collective-permute-start.9) | collective-permute-done | bytes 262176 | tf_op jit(solution)/shard_map/ppermute | solution.py:172
  34.7 0.0 collective-permute-start.12
  34.7 0.0 collective-permute-done.13.refs_5_
  34.7 2.7 %collective-permute-start.14 = (bf16[2,16,16,256]{3,2,1,0:T(8,128)(2,1)S(1)}, bf16[2,16,16,256]{3,2,1,0:T(8,128)(2,1)S(1)}, u32[]{:S(2)}, u32[]{:S(2)}) collective-permute-start(bf16[2,16,16,256]{3,2,1,0:T(8,128)(2,1)S(1)} %collective-permute-done.13.refs_5_), channel_id=1, source_target_pairs={{1,0},{2,1},{3,2},{4,3},{5,4},{6,5},{7,6},{0,7},{9,8},{10,9},{11,1... | collective-permute-start | bytes 786440 | tf_op jit(solution)/shard_map/ppermute | solution.py:172
  37.3 0.0 collective-permute-done.10.refs_6_
  37.4 1.3 %collective-permute-start.11 = (bf16[2,16,16,256]{3,2,1,0:T(8,128)(2,1)S(1)}, bf16[2,16,16,256]{3,2,1,0:T(8,128)(2,1)S(1)}, u32[]{:S(2)}, u32[]{:S(2)}) collective-permute-start(bf16[2,16,16,256]{3,2,1,0:T(8,128)(2,1)S(1)} %collective-permute-done.9.refs_4_), channel_id=1, source_target_pairs={{0,8},{1,9},{2,10},{3,11},{4,12},{5,13},{6,14},{7,15},{8,0},{9,1},... | collective-permute-start | bytes 786440 | tf_op jit(solution)/shard_map/ppermute | solution.py:172
  38.6 0.6 contract.11.refs_5_
  39.2 1.9 %collective-permute-done.12.refs_3_ = bf16[2,16,16,256]{3,2,1,0:T(8,128)(2,1)S(1)} collective-permute-done((bf16[2,16,16,256]{3,2,1,0:T(8,128)(2,1)S(1)}, bf16[2,16,16,256]{3,2,1,0:T(8,128)(2,1)S(1)}, u32[]{:S(2)}, u32[]{:S(2)}) %collective-permute-start.12) | collective-permute-done | bytes 262176 | tf_op jit(solution)/shard_map/ppermute | solution.py:172
  41.1 0.0 collective-permute-done.14.refs_4_
  41.1 0.4 contract.12.refs_3_
  41.5 0.0 copy-start.3
  41.5 0.0 copy-start.4
  41.5 0.0 copy-start.1
  41.5 0.0 copy-start.2
  41.5 1.8 %collective-permute-done.11.refs_2_ = bf16[2,16,16,256]{3,2,1,0:T(8,128)(2,1)S(1)} collective-permute-done((bf16[2,16,16,256]{3,2,1,0:T(8,128)(2,1)S(1)}, bf16[2,16,16,256]{3,2,1,0:T(8,128)(2,1)S(1)}, u32[]{:S(2)}, u32[]{:S(2)}) %collective-permute-start.11) | collective-permute-done | bytes 262176 | tf_op jit(solution)/shard_map/ppermute | solution.py:172
  43.3 1.3 %contract.13 = f32[16,8,128]{2,1,0:T(8,128)} custom-call(s32[1]{0:T(128)} %bitcast.refs_0_, bf16[2,16,32,4096]{3,2,1,0:T(8,128)(2,1)S(1)} %copy-done, bf16[2,16,16,256]{3,2,1,0:T(8,128)(2,1)S(1)} %collective-permute-done.11.refs_2_, f32[16,32,32]{2,1,0:T(8,128)S(1)} %contract.12.refs_3_), custom_call_target="tpu_custom_call" | custom-call | flops 100000000 | bytes 786432 | tf_op jit(solution)/shard_map/contract/pallas_call | solution.py:98
  44.6 12.2 %all-to-all-start = ((f32[16,8,128]{2,1,0:T(8,128)}), f32[16,8,128]{2,1,0:T(8,128)S(1)}, u32[]{:S(2)}, u32[]{:S(2)}) async-start(f32[16,8,128]{2,1,0:T(8,128)} %contract.13), calls=%async_computation | async-start | bytes 131072 | tf_op jit(solution)/shard_map/all_to_all | solution.py:178
  56.8 0.0 copy-done.3
  56.8 0.1 reshape.16.start_ref
  56.9 0.0 copy-done.4
  56.9 0.1 reshape.17.end_ref
  57.0 7.2 %all-to-all-done = f32[16,8,128]{2,1,0:T(8,128)S(1)} async-done(((f32[16,8,128]{2,1,0:T(8,128)}), f32[16,8,128]{2,1,0:T(8,128)S(1)}, u32[]{:S(2)}, u32[]{:S(2)}) %all-to-all-start) | async-done | bytes 65568 | tf_op jit(solution)/shard_map/all_to_all | solution.py:178
  64.2 0.0 copy-done.1
  64.2 0.0 copy-done.2
  64.2 1.2 %transform.1 = f32[16,2,1024]{2,1,0:T(2,128)} custom-call(f32[128,128]{1,0:T(8,128)S(1)} %bitcast.4, bf16[512,1024]{1,0:T(8,128)(2,1)S(1)} %copy-done.1, bf16[512,1024]{1,0:T(8,128)(2,1)S(1)} %copy-done.2, s32[32,1]{1,0:T(8,128)S(1)} %reshape.16.start_ref, s32[32,1]{1,0:T(8,128)S(1)} %reshape.17.end_ref), custom_call_target="tpu_custom_call" | custom-call | flops 100663296 | bytes 2097152 | tf_op jit(solution)/shard_map/transform/pallas_call | solution.py:151
Async XLA Ops:
  1.1 12.5 %collective-permute-start = (bf16[2,16,16,256]{3,2,1,0:T(8,128)(2,1)S(1)}, bf16[2,16,16,256]{3,2,1,0:T(8,128)(2,1)S(1)}, u32[]{:S(2)}, u32[]{:S(2)}) collective-permute-start(bf16[2,16,16,256]{3,2,1,0:T(8,128)(2,1)S(1)} %convert_element_type.3.refs_2_), channel_id=1, source_target_pairs={{0,1},{1,2},{2,3},{3,4},{4,5},{5,6},{6,7},{7,0},{8,9},{9,10},{10,1... | collective-permute-start | bytes 786440 | tf_op jit(solution)/shard_map/ppermute | solution.py:172
  3.6 10.0 %collective-permute-start.2 = (bf16[2,16,16,256]{3,2,1,0:T(8,128)(2,1)S(1)}, bf16[2,16,16,256]{3,2,1,0:T(8,128)(2,1)S(1)}, u32[]{:S(2)}, u32[]{:S(2)}) collective-permute-start(bf16[2,16,16,256]{3,2,1,0:T(8,128)(2,1)S(1)} %convert_element_type.3.refs_2_), channel_id=1, source_target_pairs={{1,0},{2,1},{3,2},{4,3},{5,4},{6,5},{7,6},{0,7},{9,8},{10,9},{11,1... | collective-permute-start | bytes 786440 | tf_op jit(solution)/shard_map/ppermute | solution.py:172
  7.6 8.6 %collective-permute-start.3 = (bf16[2,16,16,256]{3,2,1,0:T(8,128)(2,1)S(1)}, bf16[2,16,16,256]{3,2,1,0:T(8,128)(2,1)S(1)}, u32[]{:S(2)}, u32[]{:S(2)}) collective-permute-start(bf16[2,16,16,256]{3,2,1,0:T(8,128)(2,1)S(1)} %convert_element_type.3.refs_2_), channel_id=1, source_target_pairs={{0,8},{1,9},{2,10},{3,11},{4,12},{5,13},{6,14},{7,15},{8,0},{9,1},... | collective-permute-start | bytes 786440 | tf_op jit(solution)/shard_map/ppermute | solution.py:172
  8.9 3.4 %copy-start = (bf16[2,16,32,4096]{3,2,1,0:T(8,128)(2,1)S(1)}, bf16[2,16,32,4096]{3,2,1,0:T(8,128)(2,1)}, u32[]{:S(2)}) copy-start(bf16[2,16,32,4096]{3,2,1,0:T(8,128)(2,1)} %refs_1_.13) | copy-start | bytes 25165828
  13.6 7.8 %collective-permute-start.1 = (bf16[2,16,16,256]{3,2,1,0:T(8,128)(2,1)S(1)}, bf16[2,16,16,256]{3,2,1,0:T(8,128)(2,1)S(1)}, u32[]{:S(2)}, u32[]{:S(2)}) collective-permute-start(bf16[2,16,16,256]{3,2,1,0:T(8,128)(2,1)S(1)} %collective-permute-done.refs_4_), channel_id=1, source_target_pairs={{0,1},{1,2},{2,3},{3,4},{4,5},{5,6},{6,7},{7,0},{8,9},{9,10},{10,1... | collective-permute-start | bytes 786440 | tf_op jit(solution)/shard_map/ppermute | solution.py:172
  13.6 7.8 %collective-permute-start.7 = (bf16[2,16,16,256]{3,2,1,0:T(8,128)(2,1)S(1)}, bf16[2,16,16,256]{3,2,1,0:T(8,128)(2,1)S(1)}, u32[]{:S(2)}, u32[]{:S(2)}) collective-permute-start(bf16[2,16,16,256]{3,2,1,0:T(8,128)(2,1)S(1)} %collective-permute-done.2.refs_5_), channel_id=1, source_target_pairs={{1,0},{2,1},{3,2},{4,3},{5,4},{6,5},{7,6},{0,7},{9,8},{10,9},{11,1... | collective-permute-start | bytes 786440 | tf_op jit(solution)/shard_map/ppermute | solution.py:172
  16.3 7.8 %collective-permute-start.4 = (bf16[2,16,16,256]{3,2,1,0:T(8,128)(2,1)S(1)}, bf16[2,16,16,256]{3,2,1,0:T(8,128)(2,1)S(1)}, u32[]{:S(2)}, u32[]{:S(2)}) collective-permute-start(bf16[2,16,16,256]{3,2,1,0:T(8,128)(2,1)S(1)} %collective-permute-done.2.refs_5_), channel_id=1, source_target_pairs={{0,8},{1,9},{2,10},{3,11},{4,12},{5,13},{6,14},{7,15},{8,0},{9,1},... | collective-permute-start | bytes 786440 | tf_op jit(solution)/shard_map/ppermute | solution.py:172
  21.4 6.9 %collective-permute-start.6 = (bf16[2,16,16,256]{3,2,1,0:T(8,128)(2,1)S(1)}, bf16[2,16,16,256]{3,2,1,0:T(8,128)(2,1)S(1)}, u32[]{:S(2)}, u32[]{:S(2)}) collective-permute-start(bf16[2,16,16,256]{3,2,1,0:T(8,128)(2,1)S(1)} %collective-permute-done.1.refs_4_), channel_id=1, source_target_pairs={{0,1},{1,2},{2,3},{3,4},{4,5},{5,6},{6,7},{7,0},{8,9},{9,10},{10,1... | collective-permute-start | bytes 786440 | tf_op jit(solution)/shard_map/ppermute | solution.py:172
  21.4 6.9 %collective-permute-start.8 = (bf16[2,16,16,256]{3,2,1,0:T(8,128)(2,1)S(1)}, bf16[2,16,16,256]{3,2,1,0:T(8,128)(2,1)S(1)}, u32[]{:S(2)}, u32[]{:S(2)}) collective-permute-start(bf16[2,16,16,256]{3,2,1,0:T(8,128)(2,1)S(1)} %collective-permute-done.7.refs_5_), channel_id=1, source_target_pairs={{1,0},{2,1},{3,2},{4,3},{5,4},{6,5},{7,6},{0,7},{9,8},{10,9},{11,1... | collective-permute-start | bytes 786440 | tf_op jit(solution)/shard_map/ppermute | solution.py:172
  24.1 6.9 %collective-permute-start.5 = (bf16[2,16,16,256]{3,2,1,0:T(8,128)(2,1)S(1)}, bf16[2,16,16,256]{3,2,1,0:T(8,128)(2,1)S(1)}, u32[]{:S(2)}, u32[]{:S(2)}) collective-permute-start(bf16[2,16,16,256]{3,2,1,0:T(8,128)(2,1)S(1)} %collective-permute-done.1.refs_4_), channel_id=1, source_target_pairs={{0,8},{1,9},{2,10},{3,11},{4,12},{5,13},{6,14},{7,15},{8,0},{9,1},... | collective-permute-start | bytes 786440 | tf_op jit(solution)/shard_map/ppermute | solution.py:172
  28.2 6.4 %collective-permute-start.9 = (bf16[2,16,16,256]{3,2,1,0:T(8,128)(2,1)S(1)}, bf16[2,16,16,256]{3,2,1,0:T(8,128)(2,1)S(1)}, u32[]{:S(2)}, u32[]{:S(2)}) collective-permute-start(bf16[2,16,16,256]{3,2,1,0:T(8,128)(2,1)S(1)} %collective-permute-done.6.refs_4_), channel_id=1, source_target_pairs={{0,1},{1,2},{2,3},{3,4},{4,5},{5,6},{6,7},{7,0},{8,9},{9,10},{10,1... | collective-permute-start | bytes 786440 | tf_op jit(solution)/shard_map/ppermute | solution.py:172
  28.2 6.4 %collective-permute-start.13 = (bf16[2,16,16,256]{3,2,1,0:T(8,128)(2,1)S(1)}, bf16[2,16,16,256]{3,2,1,0:T(8,128)(2,1)S(1)}, u32[]{:S(2)}, u32[]{:S(2)}) collective-permute-start(bf16[2,16,16,256]{3,2,1,0:T(8,128)(2,1)S(1)} %collective-permute-done.4.refs_6_), channel_id=1, source_target_pairs={{1,0},{2,1},{3,2},{4,3},{5,4},{6,5},{7,6},{0,7},{9,8},{10,9},{11,1... | collective-permute-start | bytes 786440 | tf_op jit(solution)/shard_map/ppermute | solution.py:172
  30.9 6.4 %collective-permute-start.10 = (bf16[2,16,16,256]{3,2,1,0:T(8,128)(2,1)S(1)}, bf16[2,16,16,256]{3,2,1,0:T(8,128)(2,1)S(1)}, u32[]{:S(2)}, u32[]{:S(2)}) collective-permute-start(bf16[2,16,16,256]{3,2,1,0:T(8,128)(2,1)S(1)} %collective-permute-done.refs_4_), channel_id=1, source_target_pairs={{0,8},{1,9},{2,10},{3,11},{4,12},{5,13},{6,14},{7,15},{8,0},{9,1},... | collective-permute-start | bytes 786440 | tf_op jit(solution)/shard_map/ppermute | solution.py:172
  34.7 6.4 %collective-permute-start.12 = (bf16[2,16,16,256]{3,2,1,0:T(8,128)(2,1)S(1)}, bf16[2,16,16,256]{3,2,1,0:T(8,128)(2,1)S(1)}, u32[]{:S(2)}, u32[]{:S(2)}) collective-permute-start(bf16[2,16,16,256]{3,2,1,0:T(8,128)(2,1)S(1)} %collective-permute-done.5.refs_6_), channel_id=1, source_target_pairs={{0,1},{1,2},{2,3},{3,4},{4,5},{5,6},{6,7},{7,0},{8,9},{9,10},{10,1... | collective-permute-start | bytes 786440 | tf_op jit(solution)/shard_map/ppermute | solution.py:172
  34.7 6.4 %collective-permute-start.14 = (bf16[2,16,16,256]{3,2,1,0:T(8,128)(2,1)S(1)}, bf16[2,16,16,256]{3,2,1,0:T(8,128)(2,1)S(1)}, u32[]{:S(2)}, u32[]{:S(2)}) collective-permute-start(bf16[2,16,16,256]{3,2,1,0:T(8,128)(2,1)S(1)} %collective-permute-done.13.refs_5_), channel_id=1, source_target_pairs={{1,0},{2,1},{3,2},{4,3},{5,4},{6,5},{7,6},{0,7},{9,8},{10,9},{11,1... | collective-permute-start | bytes 786440 | tf_op jit(solution)/shard_map/ppermute | solution.py:172
  37.4 6.0 %collective-permute-start.11 = (bf16[2,16,16,256]{3,2,1,0:T(8,128)(2,1)S(1)}, bf16[2,16,16,256]{3,2,1,0:T(8,128)(2,1)S(1)}, u32[]{:S(2)}, u32[]{:S(2)}) collective-permute-start(bf16[2,16,16,256]{3,2,1,0:T(8,128)(2,1)S(1)} %collective-permute-done.9.refs_4_), channel_id=1, source_target_pairs={{0,8},{1,9},{2,10},{3,11},{4,12},{5,13},{6,14},{7,15},{8,0},{9,1},... | collective-permute-start | bytes 786440 | tf_op jit(solution)/shard_map/ppermute | solution.py:172
  41.5 15.3 %copy-start.3 = (s32[16,2]{0,1:T(2,128)S(1)}, s32[16,2]{0,1:T(2,128)}, u32[]{:S(2)}) copy-start(s32[16,2]{0,1:T(2,128)} %param.8) | copy-start | bytes 388
  41.5 15.4 %copy-start.4 = (s32[16,2]{0,1:T(2,128)S(1)}, s32[16,2]{0,1:T(2,128)}, u32[]{:S(2)}) copy-start(s32[16,2]{0,1:T(2,128)} %param.9) | copy-start | bytes 388
  41.5 22.7 %copy-start.1 = (bf16[512,1024]{1,0:T(8,128)(2,1)S(1)}, bf16[512,1024]{1,0:T(8,128)(2,1)}, u32[]{:S(2)}) copy-start(bf16[512,1024]{1,0:T(8,128)(2,1)} %constant.8.clone.high_ref) | copy-start | bytes 3145732
  41.5 22.6 %copy-start.2 = (bf16[512,1024]{1,0:T(8,128)(2,1)S(1)}, bf16[512,1024]{1,0:T(8,128)(2,1)}, u32[]{:S(2)}) copy-start(bf16[512,1024]{1,0:T(8,128)(2,1)} %constant.9.clone.low_ref) | copy-start | bytes 3145732
  44.6 19.6 %all-to-all-start = ((f32[16,8,128]{2,1,0:T(8,128)}), f32[16,8,128]{2,1,0:T(8,128)S(1)}, u32[]{:S(2)}, u32[]{:S(2)}) async-start(f32[16,8,128]{2,1,0:T(8,128)} %contract.13), calls=%async_computation | async-start | bytes 131072 | tf_op jit(solution)/shard_map/all_to_all | solution.py:178

commit v4 on v3

--- a/solution.py
+++ b/solution.py
@@ -24,7 +24,7 @@
     [((0, -4), (0, -3), UP), ((1, 2), (1, 1), DOWN), ((1, -1), (0, -1), ACROSS)],
     [((1, -3), (1, -2), UP), ((1, 3), (1, 2), DOWN), ((1, -4), (0, -4), ACROSS)],
 ]
-LAST = [[send[0] for send in STEPS[3]], [send[0] for send in STEPS[4][:2]], [STEPS[4][2][0]]]
+LAST = [[send[0] for send in STEPS[3]], [send[0] for send in STEPS[4]]]
 SENDS = [send for step in STEPS for send in step]
 
 COST = 0.1e9

time: 65.6 us -> 64.9 us (0.989)
  starting transfers between devices: 36 us -> 35.1 us
    ppermute x15, starting transfers between devices: 23.8 us -> 22.9 us  [per_device(): blocks[key] = lax.ppermute(value, 'recv', perm)]
    pallas_call x7 -> x6, Pallas kernels: 4.17 us -> 3.87 us  [contract(): pl.pallas_call(lambda *refs: contract_kernel(count, chunk, first, last, *...]
  transfers between devices with their start and end apart: 16 -> 16, of which waited for: 7 -> 8; matrix products, arithmetic and copies ran while one was open for 0% -> 0% of each run, Pallas kernels for 4% -> 4%
where the time goes in v4:
time: 64.9 us; the launch traced here: 64.6 us
  starting transfers between devices  35.1 us (54%)
  waiting for transfers between devices  19.7 us (30%)
  Pallas kernels  5.07 us (8%)
  local copies, waits for them, and re-layouts  3.56 us (5%)
  other arithmetic  1.07 us (2%)
    ppermute x15, starting transfers between devices, per_device(): blocks[key] = lax.ppermute(value, 'recv', perm)  22.9 us
    ppermute x15, waiting for transfers between devices, per_device(): blocks[key] = lax.ppermute(value, 'recv', perm)  12.6 us
    all_to_all x1, starting transfers between devices, per_device(): lax.all_to_all(total, 'freq', split_axis=0, concat_axis=0, tiled=True)  12.3 us
    all_to_all x1, waiting for transfers between devices, per_device(): lax.all_to_all(total, 'freq', split_axis=0, concat_axis=0, tiled=True)  7.15 us
    pallas_call x6, Pallas kernels, contract(): pl.pallas_call(lambda *refs: contract_kernel(count, chunk, first, last, *...  3.87 us
    unnamed x10, local copies, waits for them, and re-layouts  3.4 us
  transfers between devices with their start and end apart: 16, of which 8 were waited for; matrix products, arithmetic and copies ran while one was open for 0% of the time, Pallas kernels for 4%

profile of v4, /device:TPU:1, one launch (start us, length us, event | category | flops | bytes accessed | tf_op | source)
XLA Modules:
  0.0 64.6 jit_solution(17408712167755918723)
XLA Ops:
  0.0 1.1 %convert_element_type.3.refs_2_ = bf16[2,16,16,256]{3,2,1,0:T(8,128)(2,1)S(1)} convert(f32[2,16,16,256]{3,2,1,0:T(8,128)} %param.7) | non-fusion elementwise | flops 131072 | bytes 786432 | tf_op jit(solution)/shard_map/convert_element_type | solution.py:163
  1.1 2.5 %collective-permute-start = (bf16[2,16,16,256]{3,2,1,0:T(8,128)(2,1)S(1)}, bf16[2,16,16,256]{3,2,1,0:T(8,128)(2,1)S(1)}, u32[]{:S(2)}, u32[]{:S(2)}) collective-permute-start(bf16[2,16,16,256]{3,2,1,0:T(8,128)(2,1)S(1)} %convert_element_type.3.refs_2_), channel_id=1, source_target_pairs={{0,1},{1,2},{2,3},{3,4},{4,5},{5,6},{6,7},{7,0},{8,9},{9,10},{10,1... | collective-permute-start | bytes 786440 | tf_op jit(solution)/shard_map/ppermute | solution.py:172
  3.6 4.0 %collective-permute-start.2 = (bf16[2,16,16,256]{3,2,1,0:T(8,128)(2,1)S(1)}, bf16[2,16,16,256]{3,2,1,0:T(8,128)(2,1)S(1)}, u32[]{:S(2)}, u32[]{:S(2)}) collective-permute-start(bf16[2,16,16,256]{3,2,1,0:T(8,128)(2,1)S(1)} %convert_element_type.3.refs_2_), channel_id=1, source_target_pairs={{1,0},{2,1},{3,2},{4,3},{5,4},{6,5},{7,6},{0,7},{9,8},{10,9},{11,1... | collective-permute-start | bytes 786440 | tf_op jit(solution)/shard_map/ppermute | solution.py:172
  7.6 1.3 %collective-permute-start.3 = (bf16[2,16,16,256]{3,2,1,0:T(8,128)(2,1)S(1)}, bf16[2,16,16,256]{3,2,1,0:T(8,128)(2,1)S(1)}, u32[]{:S(2)}, u32[]{:S(2)}) collective-permute-start(bf16[2,16,16,256]{3,2,1,0:T(8,128)(2,1)S(1)} %convert_element_type.3.refs_2_), channel_id=1, source_target_pairs={{0,8},{1,9},{2,10},{3,11},{4,12},{5,13},{6,14},{7,15},{8,0},{9,1},... | collective-permute-start | bytes 786440 | tf_op jit(solution)/shard_map/ppermute | solution.py:172
  8.9 0.0 copy-start
  8.9 3.4 %copy-done = bf16[2,16,32,4096]{3,2,1,0:T(8,128)(2,1)S(1)} copy-done((bf16[2,16,32,4096]{3,2,1,0:T(8,128)(2,1)S(1)}, bf16[2,16,32,4096]{3,2,1,0:T(8,128)(2,1)}, u32[]{:S(2)}) %copy-start) | copy-done | bytes 8388632
  12.3 0.3 contract.6.refs_7_
  12.6 1.0 %collective-permute-done.refs_4_ = bf16[2,16,16,256]{3,2,1,0:T(8,128)(2,1)S(1)} collective-permute-done((bf16[2,16,16,256]{3,2,1,0:T(8,128)(2,1)S(1)}, bf16[2,16,16,256]{3,2,1,0:T(8,128)(2,1)S(1)}, u32[]{:S(2)}, u32[]{:S(2)}) %collective-permute-start) | collective-permute-done | bytes 262176 | tf_op jit(solution)/shard_map/ppermute | solution.py:172
  13.6 0.0 collective-permute-start.1
  13.6 0.0 collective-permute-done.2.refs_5_
  13.6 0.9 %collective-permute-done.3.refs_6_ = bf16[2,16,16,256]{3,2,1,0:T(8,128)(2,1)S(1)} collective-permute-done((bf16[2,16,16,256]{3,2,1,0:T(8,128)(2,1)S(1)}, bf16[2,16,16,256]{3,2,1,0:T(8,128)(2,1)S(1)}, u32[]{:S(2)}, u32[]{:S(2)}) %collective-permute-start.3) | collective-permute-done | bytes 262176 | tf_op jit(solution)/shard_map/ppermute | solution.py:172
  14.5 1.3 %collective-permute-start.4 = (bf16[2,16,16,256]{3,2,1,0:T(8,128)(2,1)S(1)}, bf16[2,16,16,256]{3,2,1,0:T(8,128)(2,1)S(1)}, u32[]{:S(2)}, u32[]{:S(2)}) collective-permute-start(bf16[2,16,16,256]{3,2,1,0:T(8,128)(2,1)S(1)} %collective-permute-done.2.refs_5_), channel_id=1, source_target_pairs={{0,8},{1,9},{2,10},{3,11},{4,12},{5,13},{6,14},{7,15},{8,0},{9,1},... | collective-permute-start | bytes 786440 | tf_op jit(solution)/shard_map/ppermute | solution.py:172
  15.8 1.8 %collective-permute-start.7 = (bf16[2,16,16,256]{3,2,1,0:T(8,128)(2,1)S(1)}, bf16[2,16,16,256]{3,2,1,0:T(8,128)(2,1)S(1)}, u32[]{:S(2)}, u32[]{:S(2)}) collective-permute-start(bf16[2,16,16,256]{3,2,1,0:T(8,128)(2,1)S(1)} %collective-permute-done.2.refs_5_), channel_id=1, source_target_pairs={{1,0},{2,1},{3,2},{4,3},{5,4},{6,5},{7,6},{0,7},{9,8},{10,9},{11,1... | collective-permute-start | bytes 786440 | tf_op jit(solution)/shard_map/ppermute | solution.py:172
  17.6 0.6 contract.7.refs_7_
  18.1 3.2 %collective-permute-done.1.refs_4_ = bf16[2,16,16,256]{3,2,1,0:T(8,128)(2,1)S(1)} collective-permute-done((bf16[2,16,16,256]{3,2,1,0:T(8,128)(2,1)S(1)}, bf16[2,16,16,256]{3,2,1,0:T(8,128)(2,1)S(1)}, u32[]{:S(2)}, u32[]{:S(2)}) %collective-permute-start.1) | collective-permute-done | bytes 262176 | tf_op jit(solution)/shard_map/ppermute | solution.py:172
  21.4 0.0 collective-permute-start.6
  21.4 0.0 collective-permute-done.4.refs_6_
  21.4 1.3 %collective-permute-start.5 = (bf16[2,16,16,256]{3,2,1,0:T(8,128)(2,1)S(1)}, bf16[2,16,16,256]{3,2,1,0:T(8,128)(2,1)S(1)}, u32[]{:S(2)}, u32[]{:S(2)}) collective-permute-start(bf16[2,16,16,256]{3,2,1,0:T(8,128)(2,1)S(1)} %collective-permute-done.1.refs_4_), channel_id=1, source_target_pairs={{0,8},{1,9},{2,10},{3,11},{4,12},{5,13},{6,14},{7,15},{8,0},{9,1},... | collective-permute-start | bytes 786440 | tf_op jit(solution)/shard_map/ppermute | solution.py:172
  22.7 0.0 collective-permute-done.7.refs_5_
  22.7 2.7 %collective-permute-start.8 = (bf16[2,16,16,256]{3,2,1,0:T(8,128)(2,1)S(1)}, bf16[2,16,16,256]{3,2,1,0:T(8,128)(2,1)S(1)}, u32[]{:S(2)}, u32[]{:S(2)}) collective-permute-start(bf16[2,16,16,256]{3,2,1,0:T(8,128)(2,1)S(1)} %collective-permute-done.7.refs_5_), channel_id=1, source_target_pairs={{1,0},{2,1},{3,2},{4,3},{5,4},{6,5},{7,6},{0,7},{9,8},{10,9},{11,1... | collective-permute-start | bytes 786440 | tf_op jit(solution)/shard_map/ppermute | solution.py:172
  25.4 0.6 contract.8.refs_7_
  25.9 2.3 %collective-permute-done.6.refs_4_ = bf16[2,16,16,256]{3,2,1,0:T(8,128)(2,1)S(1)} collective-permute-done((bf16[2,16,16,256]{3,2,1,0:T(8,128)(2,1)S(1)}, bf16[2,16,16,256]{3,2,1,0:T(8,128)(2,1)S(1)}, u32[]{:S(2)}, u32[]{:S(2)}) %collective-permute-start.6) | collective-permute-done | bytes 262176 | tf_op jit(solution)/shard_map/ppermute | solution.py:172
  28.2 0.0 collective-permute-start.9
  28.2 0.0 collective-permute-done.5.refs_6_
  28.2 1.3 %collective-permute-start.13 = (bf16[2,16,16,256]{3,2,1,0:T(8,128)(2,1)S(1)}, bf16[2,16,16,256]{3,2,1,0:T(8,128)(2,1)S(1)}, u32[]{:S(2)}, u32[]{:S(2)}) collective-permute-start(bf16[2,16,16,256]{3,2,1,0:T(8,128)(2,1)S(1)} %collective-permute-done.refs_4_), channel_id=1, source_target_pairs={{0,8},{1,9},{2,10},{3,11},{4,12},{5,13},{6,14},{7,15},{8,0},{9,1},... | collective-permute-start | bytes 786440 | tf_op jit(solution)/shard_map/ppermute | solution.py:172
  29.5 0.0 collective-permute-done.8.refs_5_
  29.5 2.7 %collective-permute-start.11 = (bf16[2,16,16,256]{3,2,1,0:T(8,128)(2,1)S(1)}, bf16[2,16,16,256]{3,2,1,0:T(8,128)(2,1)S(1)}, u32[]{:S(2)}, u32[]{:S(2)}) collective-permute-start(bf16[2,16,16,256]{3,2,1,0:T(8,128)(2,1)S(1)} %collective-permute-done.4.refs_6_), channel_id=1, source_target_pairs={{1,0},{2,1},{3,2},{4,3},{5,4},{6,5},{7,6},{0,7},{9,8},{10,9},{11,1... | collective-permute-start | bytes 786440 | tf_op jit(solution)/shard_map/ppermute | solution.py:172
  32.2 0.5 contract.9.refs_7_
  32.8 1.9 %collective-permute-done.9.refs_4_ = bf16[2,16,16,256]{3,2,1,0:T(8,128)(2,1)S(1)} collective-permute-done((bf16[2,16,16,256]{3,2,1,0:T(8,128)(2,1)S(1)}, bf16[2,16,16,256]{3,2,1,0:T(8,128)(2,1)S(1)}, u32[]{:S(2)}, u32[]{:S(2)}) %collective-permute-start.9) | collective-permute-done | bytes 262176 | tf_op jit(solution)/shard_map/ppermute | solution.py:172
  34.7 0.0 collective-permute-done.13.refs_6_
  34.7 1.3 %collective-permute-start.14 = (bf16[2,16,16,256]{3,2,1,0:T(8,128)(2,1)S(1)}, bf16[2,16,16,256]{3,2,1,0:T(8,128)(2,1)S(1)}, u32[]{:S(2)}, u32[]{:S(2)}) collective-permute-start(bf16[2,16,16,256]{3,2,1,0:T(8,128)(2,1)S(1)} %collective-permute-done.9.refs_4_), channel_id=1, source_target_pairs={{0,8},{1,9},{2,10},{3,11},{4,12},{5,13},{6,14},{7,15},{8,0},{9,1},... | collective-permute-start | bytes 786440 | tf_op jit(solution)/shard_map/ppermute | solution.py:172
  36.0 0.0 collective-permute-start.10
  36.0 0.0 collective-permute-done.11.refs_5_
  36.0 2.7 %collective-permute-start.12 = (bf16[2,16,16,256]{3,2,1,0:T(8,128)(2,1)S(1)}, bf16[2,16,16,256]{3,2,1,0:T(8,128)(2,1)S(1)}, u32[]{:S(2)}, u32[]{:S(2)}) collective-permute-start(bf16[2,16,16,256]{3,2,1,0:T(8,128)(2,1)S(1)} %collective-permute-done.11.refs_5_), channel_id=1, source_target_pairs={{1,0},{2,1},{3,2},{4,3},{5,4},{6,5},{7,6},{0,7},{9,8},{10,9},{11,1... | collective-permute-start | bytes 786440 | tf_op jit(solution)/shard_map/ppermute | solution.py:172
  38.6 0.6 contract.10.refs_7_
  39.2 0.0 copy-start.3
  39.2 0.0 copy-start.4
  39.2 0.0 copy-start.1
  39.2 0.0 copy-start.2
  39.2 0.7 %collective-permute-done.14.refs_6_ = bf16[2,16,16,256]{3,2,1,0:T(8,128)(2,1)S(1)} collective-permute-done((bf16[2,16,16,256]{3,2,1,0:T(8,128)(2,1)S(1)}, bf16[2,16,16,256]{3,2,1,0:T(8,128)(2,1)S(1)}, u32[]{:S(2)}, u32[]{:S(2)}) %collective-permute-start.14) | collective-permute-done | bytes 262176 | tf_op jit(solution)/shard_map/ppermute | solution.py:172
  39.9 2.5 %collective-permute-done.10.refs_4_ = bf16[2,16,16,256]{3,2,1,0:T(8,128)(2,1)S(1)} collective-permute-done((bf16[2,16,16,256]{3,2,1,0:T(8,128)(2,1)S(1)}, bf16[2,16,16,256]{3,2,1,0:T(8,128)(2,1)S(1)}, u32[]{:S(2)}, u32[]{:S(2)}) %collective-permute-start.10) | collective-permute-done | bytes 262176 | tf_op jit(solution)/shard_map/ppermute | solution.py:172
  42.4 0.0 collective-permute-done.12.refs_5_
  42.4 1.4 %contract.11 = f32[16,8,128]{2,1,0:T(8,128)} custom-call(s32[1]{0:T(128)} %bitcast.refs_0_, bf16[2,16,32,4096]{3,2,1,0:T(8,128)(2,1)S(1)} %copy-done, bf16[2,16,32,4096]{3,2,1,0:T(8,128)(2,1)S(1)} %copy-done, bf16[2,16,32,4096]{3,2,1,0:T(8,128)(2,1)S(1)} %copy-done, bf16[2,16,16,256]{3,2,1,0:T(8,128)(2,1)S(1)} %collective-permute-done.10.refs_4_, ...), custom_call_target="tpu_custom_call" | custom-call | flops 300000000 | bytes 2359296 | tf_op jit(solution)/shard_map/contract/pallas_call | solution.py:98
  43.8 12.3 %all-to-all-start = ((f32[16,8,128]{2,1,0:T(8,128)}), f32[16,8,128]{2,1,0:T(8,128)S(1)}, u32[]{:S(2)}, u32[]{:S(2)}) async-start(f32[16,8,128]{2,1,0:T(8,128)} %contract.11), calls=%async_computation | async-start | bytes 131072 | tf_op jit(solution)/shard_map/all_to_all | solution.py:178
  56.1 0.0 copy-done.3
  56.1 0.1 reshape.16.start_ref
  56.2 0.0 copy-done.4
  56.2 0.1 reshape.17.end_ref
  56.3 7.2 %all-to-all-done = f32[16,8,128]{2,1,0:T(8,128)S(1)} async-done(((f32[16,8,128]{2,1,0:T(8,128)}), f32[16,8,128]{2,1,0:T(8,128)S(1)}, u32[]{:S(2)}, u32[]{:S(2)}) %all-to-all-start) | async-done | bytes 65568 | tf_op jit(solution)/shard_map/all_to_all | solution.py:178
  63.4 0.0 copy-done.1
  63.4 0.0 copy-done.2
  63.4 1.2 %transform.1 = f32[16,2,1024]{2,1,0:T(2,128)} custom-call(f32[128,128]{1,0:T(8,128)S(1)} %bitcast.4, bf16[512,1024]{1,0:T(8,128)(2,1)S(1)} %copy-done.1, bf16[512,1024]{1,0:T(8,128)(2,1)S(1)} %copy-done.2, s32[32,1]{1,0:T(8,128)S(1)} %reshape.16.start_ref, s32[32,1]{1,0:T(8,128)S(1)} %reshape.17.end_ref), custom_call_target="tpu_custom_call" | custom-call | flops 100663296 | bytes 2097152 | tf_op jit(solution)/shard_map/transform/pallas_call | solution.py:151
Async XLA Ops:
  1.1 12.5 %collective-permute-start = (bf16[2,16,16,256]{3,2,1,0:T(8,128)(2,1)S(1)}, bf16[2,16,16,256]{3,2,1,0:T(8,128)(2,1)S(1)}, u32[]{:S(2)}, u32[]{:S(2)}) collective-permute-start(bf16[2,16,16,256]{3,2,1,0:T(8,128)(2,1)S(1)} %convert_element_type.3.refs_2_), channel_id=1, source_target_pairs={{0,1},{1,2},{2,3},{3,4},{4,5},{5,6},{6,7},{7,0},{8,9},{9,10},{10,1... | collective-permute-start | bytes 786440 | tf_op jit(solution)/shard_map/ppermute | solution.py:172
  3.6 10.0 %collective-permute-start.2 = (bf16[2,16,16,256]{3,2,1,0:T(8,128)(2,1)S(1)}, bf16[2,16,16,256]{3,2,1,0:T(8,128)(2,1)S(1)}, u32[]{:S(2)}, u32[]{:S(2)}) collective-permute-start(bf16[2,16,16,256]{3,2,1,0:T(8,128)(2,1)S(1)} %convert_element_type.3.refs_2_), channel_id=1, source_target_pairs={{1,0},{2,1},{3,2},{4,3},{5,4},{6,5},{7,6},{0,7},{9,8},{10,9},{11,1... | collective-permute-start | bytes 786440 | tf_op jit(solution)/shard_map/ppermute | solution.py:172
  7.6 6.9 %collective-permute-start.3 = (bf16[2,16,16,256]{3,2,1,0:T(8,128)(2,1)S(1)}, bf16[2,16,16,256]{3,2,1,0:T(8,128)(2,1)S(1)}, u32[]{:S(2)}, u32[]{:S(2)}) collective-permute-start(bf16[2,16,16,256]{3,2,1,0:T(8,128)(2,1)S(1)} %convert_element_type.3.refs_2_), channel_id=1, source_target_pairs={{0,8},{1,9},{2,10},{3,11},{4,12},{5,13},{6,14},{7,15},{8,0},{9,1},... | collective-permute-start | bytes 786440 | tf_op jit(solution)/shard_map/ppermute | solution.py:172
  8.9 3.4 %copy-start = (bf16[2,16,32,4096]{3,2,1,0:T(8,128)(2,1)S(1)}, bf16[2,16,32,4096]{3,2,1,0:T(8,128)(2,1)}, u32[]{:S(2)}) copy-start(bf16[2,16,32,4096]{3,2,1,0:T(8,128)(2,1)} %refs_3_.9) | copy-start | bytes 25165828
  13.6 7.8 %collective-permute-start.1 = (bf16[2,16,16,256]{3,2,1,0:T(8,128)(2,1)S(1)}, bf16[2,16,16,256]{3,2,1,0:T(8,128)(2,1)S(1)}, u32[]{:S(2)}, u32[]{:S(2)}) collective-permute-start(bf16[2,16,16,256]{3,2,1,0:T(8,128)(2,1)S(1)} %collective-permute-done.refs_4_), channel_id=1, source_target_pairs={{0,1},{1,2},{2,3},{3,4},{4,5},{5,6},{6,7},{7,0},{8,9},{9,10},{10,1... | collective-permute-start | bytes 786440 | tf_op jit(solution)/shard_map/ppermute | solution.py:172
  14.5 6.9 %collective-permute-start.4 = (bf16[2,16,16,256]{3,2,1,0:T(8,128)(2,1)S(1)}, bf16[2,16,16,256]{3,2,1,0:T(8,128)(2,1)S(1)}, u32[]{:S(2)}, u32[]{:S(2)}) collective-permute-start(bf16[2,16,16,256]{3,2,1,0:T(8,128)(2,1)S(1)} %collective-permute-done.2.refs_5_), channel_id=1, source_target_pairs={{0,8},{1,9},{2,10},{3,11},{4,12},{5,13},{6,14},{7,15},{8,0},{9,1},... | collective-permute-start | bytes 786440 | tf_op jit(solution)/shard_map/ppermute | solution.py:172
  15.8 6.9 %collective-permute-start.7 = (bf16[2,16,16,256]{3,2,1,0:T(8,128)(2,1)S(1)}, bf16[2,16,16,256]{3,2,1,0:T(8,128)(2,1)S(1)}, u32[]{:S(2)}, u32[]{:S(2)}) collective-permute-start(bf16[2,16,16,256]{3,2,1,0:T(8,128)(2,1)S(1)} %collective-permute-done.2.refs_5_), channel_id=1, source_target_pairs={{1,0},{2,1},{3,2},{4,3},{5,4},{6,5},{7,6},{0,7},{9,8},{10,9},{11,1... | collective-permute-start | bytes 786440 | tf_op jit(solution)/shard_map/ppermute | solution.py:172
  21.4 6.9 %collective-permute-start.6 = (bf16[2,16,16,256]{3,2,1,0:T(8,128)(2,1)S(1)}, bf16[2,16,16,256]{3,2,1,0:T(8,128)(2,1)S(1)}, u32[]{:S(2)}, u32[]{:S(2)}) collective-permute-start(bf16[2,16,16,256]{3,2,1,0:T(8,128)(2,1)S(1)} %collective-permute-done.1.refs_4_), channel_id=1, source_target_pairs={{0,1},{1,2},{2,3},{3,4},{4,5},{5,6},{6,7},{7,0},{8,9},{9,10},{10,1... | collective-permute-start | bytes 786440 | tf_op jit(solution)/shard_map/ppermute | solution.py:172
  21.4 6.9 %collective-permute-start.5 = (bf16[2,16,16,256]{3,2,1,0:T(8,128)(2,1)S(1)}, bf16[2,16,16,256]{3,2,1,0:T(8,128)(2,1)S(1)}, u32[]{:S(2)}, u32[]{:S(2)}) collective-permute-start(bf16[2,16,16,256]{3,2,1,0:T(8,128)(2,1)S(1)} %collective-permute-done.1.refs_4_), channel_id=1, source_target_pairs={{0,8},{1,9},{2,10},{3,11},{4,12},{5,13},{6,14},{7,15},{8,0},{9,1},... | collective-permute-start | bytes 786440 | tf_op jit(solution)/shard_map/ppermute | solution.py:172
  22.7 6.9 %collective-permute-start.8 = (bf16[2,16,16,256]{3,2,1,0:T(8,128)(2,1)S(1)}, bf16[2,16,16,256]{3,2,1,0:T(8,128)(2,1)S(1)}, u32[]{:S(2)}, u32[]{:S(2)}) collective-permute-start(bf16[2,16,16,256]{3,2,1,0:T(8,128)(2,1)S(1)} %collective-permute-done.7.refs_5_), channel_id=1, source_target_pairs={{1,0},{2,1},{3,2},{4,3},{5,4},{6,5},{7,6},{0,7},{9,8},{10,9},{11,1... | collective-permute-start | bytes 786440 | tf_op jit(solution)/shard_map/ppermute | solution.py:172
  28.2 6.4 %collective-permute-start.9 = (bf16[2,16,16,256]{3,2,1,0:T(8,128)(2,1)S(1)}, bf16[2,16,16,256]{3,2,1,0:T(8,128)(2,1)S(1)}, u32[]{:S(2)}, u32[]{:S(2)}) collective-permute-start(bf16[2,16,16,256]{3,2,1,0:T(8,128)(2,1)S(1)} %collective-permute-done.6.refs_4_), channel_id=1, source_target_pairs={{0,1},{1,2},{2,3},{3,4},{4,5},{5,6},{6,7},{7,0},{8,9},{9,10},{10,1... | collective-permute-start | bytes 786440 | tf_op jit(solution)/shard_map/ppermute | solution.py:172
  28.2 6.4 %collective-permute-start.13 = (bf16[2,16,16,256]{3,2,1,0:T(8,128)(2,1)S(1)}, bf16[2,16,16,256]{3,2,1,0:T(8,128)(2,1)S(1)}, u32[]{:S(2)}, u32[]{:S(2)}) collective-permute-start(bf16[2,16,16,256]{3,2,1,0:T(8,128)(2,1)S(1)} %collective-permute-done.refs_4_), channel_id=1, source_target_pairs={{0,8},{1,9},{2,10},{3,11},{4,12},{5,13},{6,14},{7,15},{8,0},{9,1},... | collective-permute-start | bytes 786440 | tf_op jit(solution)/shard_map/ppermute | solution.py:172
  29.5 6.4 %collective-permute-start.11 = (bf16[2,16,16,256]{3,2,1,0:T(8,128)(2,1)S(1)}, bf16[2,16,16,256]{3,2,1,0:T(8,128)(2,1)S(1)}, u32[]{:S(2)}, u32[]{:S(2)}) collective-permute-start(bf16[2,16,16,256]{3,2,1,0:T(8,128)(2,1)S(1)} %collective-permute-done.4.refs_6_), channel_id=1, source_target_pairs={{1,0},{2,1},{3,2},{4,3},{5,4},{6,5},{7,6},{0,7},{9,8},{10,9},{11,1... | collective-permute-start | bytes 786440 | tf_op jit(solution)/shard_map/ppermute | solution.py:172
  34.7 5.2 %collective-permute-start.14 = (bf16[2,16,16,256]{3,2,1,0:T(8,128)(2,1)S(1)}, bf16[2,16,16,256]{3,2,1,0:T(8,128)(2,1)S(1)}, u32[]{:S(2)}, u32[]{:S(2)}) collective-permute-start(bf16[2,16,16,256]{3,2,1,0:T(8,128)(2,1)S(1)} %collective-permute-done.9.refs_4_), channel_id=1, source_target_pairs={{0,8},{1,9},{2,10},{3,11},{4,12},{5,13},{6,14},{7,15},{8,0},{9,1},... | collective-permute-start | bytes 786440 | tf_op jit(solution)/shard_map/ppermute | solution.py:172
  36.0 6.4 %collective-permute-start.10 = (bf16[2,16,16,256]{3,2,1,0:T(8,128)(2,1)S(1)}, bf16[2,16,16,256]{3,2,1,0:T(8,128)(2,1)S(1)}, u32[]{:S(2)}, u32[]{:S(2)}) collective-permute-start(bf16[2,16,16,256]{3,2,1,0:T(8,128)(2,1)S(1)} %collective-permute-done.5.refs_6_), channel_id=1, source_target_pairs={{0,1},{1,2},{2,3},{3,4},{4,5},{5,6},{6,7},{7,0},{8,9},{9,10},{10,1... | collective-permute-start | bytes 786440 | tf_op jit(solution)/shard_map/ppermute | solution.py:172
  36.0 6.5 %collective-permute-start.12 = (bf16[2,16,16,256]{3,2,1,0:T(8,128)(2,1)S(1)}, bf16[2,16,16,256]{3,2,1,0:T(8,128)(2,1)S(1)}, u32[]{:S(2)}, u32[]{:S(2)}) collective-permute-start(bf16[2,16,16,256]{3,2,1,0:T(8,128)(2,1)S(1)} %collective-permute-done.11.refs_5_), channel_id=1, source_target_pairs={{1,0},{2,1},{3,2},{4,3},{5,4},{6,5},{7,6},{0,7},{9,8},{10,9},{11,1... | collective-permute-start | bytes 786440 | tf_op jit(solution)/shard_map/ppermute | solution.py:172
  39.2 16.9 %copy-start.3 = (s32[16,2]{0,1:T(2,128)S(1)}, s32[16,2]{0,1:T(2,128)}, u32[]{:S(2)}) copy-start(s32[16,2]{0,1:T(2,128)} %param.8) | copy-start | bytes 388
  39.2 17.0 %copy-start.4 = (s32[16,2]{0,1:T(2,128)S(1)}, s32[16,2]{0,1:T(2,128)}, u32[]{:S(2)}) copy-start(s32[16,2]{0,1:T(2,128)} %param.9) | copy-start | bytes 388
  39.2 24.2 %copy-start.1 = (bf16[512,1024]{1,0:T(8,128)(2,1)S(1)}, bf16[512,1024]{1,0:T(8,128)(2,1)}, u32[]{:S(2)}) copy-start(bf16[512,1024]{1,0:T(8,128)(2,1)} %constant.8.clone.high_ref) | copy-start | bytes 3145732
  39.2 24.2 %copy-start.2 = (bf16[512,1024]{1,0:T(8,128)(2,1)S(1)}, bf16[512,1024]{1,0:T(8,128)(2,1)}, u32[]{:S(2)}) copy-start(bf16[512,1024]{1,0:T(8,128)(2,1)} %constant.9.clone.low_ref) | copy-start | bytes 3145732
  43.8 19.6 %all-to-all-start = ((f32[16,8,128]{2,1,0:T(8,128)}), f32[16,8,128]{2,1,0:T(8,128)S(1)}, u32[]{:S(2)}, u32[]{:S(2)}) async-start(f32[16,8,128]{2,1,0:T(8,128)} %contract.11), calls=%async_computation | async-start | bytes 131072 | tf_op jit(solution)/shard_map/all_to_all | solution.py:178
